TPU v7x, 512 devices: a whole 4x4x16 slice. The times are simulated.
512 devices in a mesh: seq: 64 (over y, z), kvh: 8 (over x, core).
Axes of the slice: x: 4, y: 4, z: 16, core: 2. Of those that a mesh axis runs over, the one named last changes fastest.
Arguments:
- resid: bfloat16 [64, 2, 8192], P(None, None, 'seq'), may hold values from -6 to 6
- queries: bfloat16 [64, 2, 64, 128], P(None, None, 'kvh'), may hold values from -200 to 200
- new_kv: bfloat16 [2, 64, 2, 8, 128], P(None, 'seq', None, 'kvh'), may hold values from -9 to 9
- prefix_cache: bfloat16 [2, 32768, 8, 128], P(None, 'seq', 'kvh'), may hold values from -16 to 16
- suffix_cache: bfloat16 [2, 64, 256, 8, 128], P(None, 'seq', None, 'kvh'), may hold values from -8 to 8
- suffix_lengths: int32 [64], replicated, may hold values from 1 to 256, 8192 in all
- out_weight: bfloat16 [8192, 8192], P('kvh', 'seq'), may hold values from -0.0625 to 0.0625
- norm_gain: float32 [8192], replicated, may hold values from 0.5 to 1.5
- gate_up: bfloat16 [2, 8192, 8, 3584], P(None, None, 'kvh', 'seq'), may hold values from -0.0625 to 0.0625
- down_weight: bfloat16 [28672, 8192], P('kvh', 'seq'), may hold values from -0.03125 to 0.03125
Outputs:
- layer_out: bfloat16 [64, 2, 8192], P(None, None, ('seq', 'kvh'))
Inputs may be any that keep to these rules, and one draw needn't show every extreme that they name: `suffix_lengths`: the lengths sum to 8192.
All inputs are finite; a program needn't handle non-finite values.
Results may differ from a plain program's by a relative error of at most 0.02.
Values may be sent and summed in bfloat16 or wider, within the bound.
A program may use at most 128 MiB of HBM per device.

v0:
```python
import math

import jax
import jax.numpy as jnp
from jax import lax
from jax.sharding import PartitionSpec as P

theta_base = 500000.0
ntk_factor = 4.0
norm_eps = 1e-05
masked_score = -1e30


def joined(value, axis, combine):
    everything = jax.tree.map(lambda part: lax.all_gather(part, axis), value)
    leading = jax.tree.map(lambda part: part[0], everything)

    def hop(k, so_far):
        return combine(so_far, jax.tree.map(lambda part: part[k], everything))

    return lax.fori_loop(1, lax.axis_size(axis), hop, leading)


def rotary_tables(lengths, prefix_len, head_dim, step_count):
    step_index = jnp.arange(step_count, dtype=jnp.int32)
    position = (prefix_len + lengths[:, None] + step_index[None, :]).astype(jnp.float32)
    anchor = float(prefix_len // 4)
    growth = ntk_factor * (position + 1.0) / anchor - (ntk_factor - 1.0)
    log_base = math.log(theta_base) + head_dim / (head_dim - 2.0) * jnp.log(growth)
    exponent = -2.0 * jnp.arange(head_dim // 2, dtype=jnp.float32) / head_dim
    angles = position[..., None] * jnp.exp(log_base[..., None] * exponent)
    return (jnp.cos(angles), jnp.sin(angles))


def rotate(values, cos_table, sin_table):
    half_dim = values.shape[-1] // 2
    widened = values.astype(jnp.float32)
    first_half = widened[..., :half_dim]
    second = widened[..., half_dim:]
    return jnp.concatenate(
        [first_half * cos_table - second * sin_table, second * cos_table + first_half * sin_table],
        axis=-1,
    ).astype(jnp.bfloat16)


def combine(earlier, later):
    joint_peak = jnp.maximum(earlier[0], later[0])
    left_factor = jnp.exp(earlier[0] - joint_peak)
    right_factor = jnp.exp(later[0] - joint_peak)
    return (
        joint_peak,
        earlier[1] * left_factor + later[1] * right_factor,
        earlier[2] * left_factor[..., None] + later[2] * right_factor[..., None],
    )


def body(
    resid,
    queries,
    new_kv,
    prefix_cache,
    suffix_cache,
    suffix_lengths,
    out_weight,
    norm_gain,
    gate_up,
    down_weight,
):
    seq_count = lax.axis_size("seq")
    kvh_count = lax.axis_size("kvh")
    seq_index = lax.axis_index("seq")
    kvh_index = lax.axis_index("kvh")
    requests, step_count, local_heads, head_dim = queries.shape
    local_kv = prefix_cache.shape[2]
    group_size = local_heads // local_kv
    owned_rows = new_kv.shape[1]
    suffix_max = suffix_cache.shape[2]
    prefix_len = prefix_cache.shape[1] * seq_count
    score_scale = 1.0 / math.sqrt(head_dim)
    cos_table, sin_table = rotary_tables(suffix_lengths, prefix_len, head_dim, step_count)
    rotated = rotate(queries, cos_table[:, :, None, :], sin_table[:, :, None, :])
    grouped = rotated.reshape(requests, step_count, local_kv, group_size, head_dim)
    scores = (
        jnp.einsum("rtkgd,nkd->rtkgn", grouped, prefix_cache[0], preferred_element_type=jnp.float32)
        * score_scale
    )
    block_peak = jnp.max(scores, axis=-1)
    weights = jnp.exp(scores - block_peak[..., None])
    block_total = jnp.sum(weights, axis=-1)
    block_acc = jnp.einsum(
        "rtkgn,nkd->rtkgd",
        weights.astype(jnp.bfloat16),
        prefix_cache[1],
        preferred_element_type=jnp.float32,
    )
    first_row = seq_index * owned_rows
    own_queries = lax.dynamic_slice_in_dim(grouped, first_row, owned_rows, 0)
    own_cos = lax.dynamic_slice_in_dim(cos_table, first_row, owned_rows, 0)
    own_sin = lax.dynamic_slice_in_dim(sin_table, first_row, owned_rows, 0)
    own_lengths = lax.dynamic_slice_in_dim(suffix_lengths, first_row, owned_rows, 0)
    new_keys = rotate(new_kv[0], own_cos[:, :, None, :], own_sin[:, :, None, :])
    suf_scores = (
        jnp.einsum(
            "rtkgd,rnkd->rtkgn", own_queries, suffix_cache[0], preferred_element_type=jnp.float32
        )
        * score_scale
    )
    suffix_live = jnp.arange(suffix_max, dtype=jnp.int32)[None, :] < own_lengths[:, None]
    suf_scores = jnp.where(suffix_live[:, None, None, None, :], suf_scores, masked_score)
    new_scores = (
        jnp.einsum("rtkgd,rukd->rtkgu", own_queries, new_keys, preferred_element_type=jnp.float32)
        * score_scale
    )
    causal = (
        jnp.arange(step_count, dtype=jnp.int32)[None, :]
        <= jnp.arange(step_count, dtype=jnp.int32)[:, None]
    )
    new_scores = jnp.where(causal[None, :, None, None, :], new_scores, masked_score)
    suf_peak = jnp.maximum(jnp.max(suf_scores, axis=-1), jnp.max(new_scores, axis=-1))
    suf_weights = jnp.exp(suf_scores - suf_peak[..., None])
    new_weights = jnp.exp(new_scores - suf_peak[..., None])
    suf_total = jnp.sum(suf_weights, axis=-1) + jnp.sum(new_weights, axis=-1)
    suf_acc = jnp.einsum(
        "rtkgn,rnkd->rtkgd",
        suf_weights.astype(jnp.bfloat16),
        suffix_cache[1],
        preferred_element_type=jnp.float32,
    )
    suf_acc = suf_acc + jnp.einsum(
        "rtkgu,rukd->rtkgd",
        new_weights.astype(jnp.bfloat16),
        new_kv[1],
        preferred_element_type=jnp.float32,
    )
    local_parts = (block_peak, block_total, block_acc)
    own_parts = tuple(
        (lax.dynamic_slice_in_dim(whole, first_row, owned_rows, 0) for whole in local_parts)
    )
    own_joint = combine(own_parts, (suf_peak, suf_total, suf_acc))
    contrib = tuple(
        (
            lax.dynamic_update_slice_in_dim(whole, piece_own, first_row, 0)
            for whole, piece_own in zip(local_parts, own_joint)
        )
    )
    merged = joined(contrib, "seq", combine)
    attention = (
        (merged[2] / merged[1][..., None])
        .astype(jnp.bfloat16)
        .reshape(requests, step_count, local_heads * head_dim)
    )
    projected = jnp.einsum("rtc,cd->rtd", attention, out_weight, preferred_element_type=jnp.float32)
    summed = lax.psum(projected.astype(jnp.bfloat16), "kvh").astype(jnp.float32)
    stream_local = (resid.astype(jnp.float32) + summed).astype(jnp.bfloat16)
    stream = lax.all_gather(stream_local, "seq", axis=2, tiled=True)
    model_width = stream.shape[2]
    stream_wide = stream.reshape(requests * step_count, model_width).astype(jnp.float32)
    inv_rms = lax.rsqrt(jnp.mean(stream_wide * stream_wide, axis=-1, keepdims=True) + norm_eps)
    normed = (stream_wide * inv_rms * norm_gain[None, :]).astype(jnp.bfloat16)
    gate_part = jnp.dot(normed, gate_up[0, :, 0, :], preferred_element_type=jnp.float32)
    up_part = jnp.dot(normed, gate_up[1, :, 0, :], preferred_element_type=jnp.float32)
    hidden = (jax.nn.silu(gate_part) * up_part).astype(jnp.bfloat16)
    ffn_part = jnp.dot(
        lax.all_gather(hidden, "seq", axis=1, tiled=True),
        down_weight,
        preferred_element_type=jnp.float32,
    )
    ffn_share = lax.psum_scatter(
        ffn_part.astype(jnp.bfloat16), "kvh", scatter_dimension=1, tiled=True
    ).astype(jnp.float32)
    out_width = ffn_share.shape[1]
    column = (seq_index * kvh_count + kvh_index) * out_width
    stream_share = lax.dynamic_slice_in_dim(stream_wide, column, out_width, 1)
    return (stream_share + ffn_share).astype(jnp.bfloat16).reshape(requests, step_count, out_width)


def solution(mesh):
    placed = (
        P(None, None, "seq"),
        P(None, None, "kvh", None),
        P(None, "seq", None, "kvh", None),
        P(None, "seq", "kvh", None),
        P(None, "seq", None, "kvh", None),
        P(),
        P("kvh", "seq"),
        P(),
        P(None, None, "kvh", "seq"),
        P("kvh", "seq"),
    )
    return jax.shard_map(
        body, mesh=mesh, in_specs=placed, out_specs=P(None, None, ("seq", "kvh")), check_vma=False
    )
```

profile of v0, /device:TPU:1, one launch (start us, length us, event | category | flops | bytes accessed | tf_op | source)
XLA Modules:
  0.0 741.6 jit_solution(11657712402362588622)
XLA Ops:
  18.3 88.7 %all_gather.27 = f32[64,64,2,1,8]{1,4,3,2,0:T(8,128)S(1)} all-gather(f32[1,64,2,1,8]{1,4,3,2,0:T(8,128)S(1)} %copy.77), channel_id=1, replica_groups=mesh['seq'=64,'kvh'=8] {'seq'}, dimensions={0}, use_global_device_ids=true | all-gather | bytes 266240 | tf_op jit(solution)/shard_map/all_gather | solution.py:15
  107.1 83.3 %all_gather.29 = f32[64,64,2,1,8]{1,4,3,2,0:T(8,128)S(1)} all-gather(f32[1,64,2,1,8]{1,4,3,2,0:T(8,128)S(1)} %copy.82), channel_id=1, replica_groups=mesh['seq'=64,'kvh'=8] {'seq'}, dimensions={0}, use_global_device_ids=true | all-gather | bytes 266240 | tf_op jit(solution)/shard_map/all_gather | solution.py:15
  190.4 128.2 %all-gather.3.cloned.1.call-done = f32[64,64,2,1,8,128]{5,4,3,2,1,0:T(8,128)} async-done(((f32[1,64,2,1,8,128]{5,4,3,2,1,0:T(8,128)}), f32[64,64,2,1,8,128]{5,4,3,2,1,0:T(8,128)}) %all-gather.3.cloned.1.call-update) | async-done | bytes 33554448 | tf_op jit(solution)/shard_map/all_gather | solution.py:15
  319.6 109.6 %while.19 = (s32[]{:T(128)}, f32[64,2,1,8]{0,3,2,1:T(8,128)S(1)}, f32[64,2,1,8]{0,3,2,1:T(8,128)S(1)}, f32[64,2,1,8,128]{4,3,2,1,0:T(8,128)S(1)}, f32[64,64,2,1,...) while((s32[]{:T(128)}, f32[64,2,1,8]{0,3,2,1:T(8,128)S(1)}, ...), condition=%wide.region_7.8_spmd, body=%wide.region_6.7_spmd.sunk | while | flops 400389 | bytes 1650835 | solution.py:21
  319.9 1.4 fusion.87
  321.7 1.4 fusion.87
  323.4 1.4 fusion.87
  325.2 1.4 fusion.87
  326.9 1.4 fusion.87
  328.6 1.4 fusion.87
  330.4 1.4 fusion.87
  332.1 1.4 fusion.87
  333.9 1.4 fusion.87
  335.6 1.4 fusion.87
  337.3 1.4 fusion.87
  339.1 1.4 fusion.87
  340.8 1.4 fusion.87
  342.6 1.4 fusion.87
  344.3 1.4 fusion.87
  346.0 1.4 fusion.87
  347.8 1.4 fusion.87
  349.5 1.4 fusion.87
  351.3 1.4 fusion.87
  353.0 1.4 fusion.87
  354.7 1.4 fusion.87
  356.5 1.4 fusion.87
  358.2 1.4 fusion.87
  360.0 1.4 fusion.87
  361.7 1.4 fusion.87
  363.4 1.4 fusion.87
  365.2 1.4 fusion.87
  366.9 1.4 fusion.87
  368.7 1.4 fusion.87
  370.4 1.4 fusion.87
  372.1 1.4 fusion.87
  373.9 1.4 fusion.87
  375.6 1.4 fusion.87
  429.9 22.7 %psum.7 = bf16[64,2,128]{2,0,1:T(8,128)(2,1)S(1)} all-reduce(bf16[64,2,128]{2,0,1:T(8,128)(2,1)S(1)} %convolution_convert_fusion.1), channel_id=1, replica_groups=mesh['seq'=64,'kvh'=8] {'kvh'}, use_global_device_ids=true, to_apply=%region_8.9 | all-reduce | flops 16384 | bytes 65536 | tf_op jit(solution)/shard_map/psum | solution.py:153
  453.3 122.9 %all-gather.5.cloned.1.call-done = bf16[64,2,8192]{2,0,1:T(8,128)(2,1)} async-done(((bf16[64,2,128]{2,0,1:T(8,128)(2,1)}), bf16[64,2,8192]{2,0,1:T(8,128)(2,1)}) %all-gather.5.cloned.1.call-update) | async-done | bytes 2097168 | tf_op jit(solution)/shard_map/all_gather | solution.py:155
  576.3 2.3 multiply_reduce_fusion
  579.1 3.5 copy.96
  582.6 4.1 convert_element_type.104
  586.8 2.8 fusion.24
  589.5 2.0 fusion.8
  591.5 74.6 %all_gather.34 = bf16[128,3584]{0,1:T(8,128)(2,1)S(1)} all-gather(bf16[128,56]{0,1:T(8,128)(2,1)S(1)} %fusion.8), channel_id=1, replica_groups=mesh['seq'=64,'kvh'=8] {'seq'}, dimensions={1}, use_global_device_ids=true | all-gather | bytes 931840 | tf_op jit(solution)/shard_map/all_gather | solution.py:164
  667.2 4.1 copy.94
  671.3 6.1 reshape.390
  678.4 55.2 %reduce-scatter.2.cloned.1.call-done = bf16[128,16]{0,1:T(8,128)(2,1)} async-done(((bf16[128,128]{0,1:T(8,128)(2,1)}), bf16[128,16]{0,1:T(8,128)(2,1)}) %reduce-scatter.2.cloned.1.call-update) | async-done | bytes 4112 | tf_op jit(solution)/shard_map/reduce_scatter | solution.py:168
  (430 shorter events, 76.4 us)
Async XLA Ops:
  6.5 659.6 %copy-start = (bf16[3584,128]{1,0:T(8,128)(2,1)S(1)}, bf16[3584,128]{1,0:T(8,128)(2,1)}, u32[]{:S(2)}) copy-start(bf16[3584,128]{1,0:T(8,128)(2,1)} %param.21) | copy-start | bytes 2752516
  6.5 6.2 copy-start.7
  6.5 312.0 %all-gather.3.cloned.1.call-start = ((), (), s32[]{:S(2)}) async-start(), calls=%async_computation.1 | async-start | bytes 34078720 | tf_op jit(solution)/shard_map/all_gather | solution.py:15
  12.6 1.0 copy-start.10
  13.4 1.9 copy-start.4
  13.9 1.3 copy-start.11
  14.7 0.7 copy-start.14
  15.6 0.9 copy-start.3
  16.5 1.5 copy-start.5
  16.5 1.5 copy-start.12
  16.5 1.7 copy-start.13
  16.5 559.8 %all-gather.5.cloned.1.call-start = ((), (), s32[]{:S(2)}) async-start(), calls=%async_computation.2 | async-start | bytes 2129920 | tf_op jit(solution)/shard_map/all_gather | solution.py:155
  319.6 110.1 %copy-start.6 = (bf16[1024,128]{1,0:T(8,128)(2,1)S(1)}, bf16[1024,128]{1,0:T(8,128)(2,1)}, u32[]{:S(2)}) copy-start(bf16[1024,128]{1,0:T(8,128)(2,1)} %param.18) | copy-start | bytes 786436
  429.3 23.4 %copy-start.9 = (bf16[64,2,128]{2,1,0:T(2,128)(2,1)S(1)}, bf16[64,2,128]{2,1,0:T(2,128)(2,1)}, u32[]{:S(2)}) copy-start(bf16[64,2,128]{2,1,0:T(2,128)(2,1)} %param.12) | copy-start | bytes 98308
  429.4 149.1 %copy-start.8 = (f32[8192]{0:T(1024)S(1)}, f32[8192]{0:T(1024)}, u32[]{:S(2)}) copy-start(f32[8192]{0:T(1024)} %param.19) | copy-start | bytes 98308
  453.3 280.3 %reduce-scatter.2.cloned.1.call-start = ((), (), s32[]{:S(2)}) async-start(), calls=%async_computation.3 | async-start | bytes 36864 | tf_op jit(solution)/shard_map/reduce_scatter | solution.py:168
  576.3 2.3 copy-start.1
  586.7 2.8 copy-start.2
Sparse Core Ops, SparseCore 0:
  16.6 301.9 all-gather.2
  453.4 122.8 all-gather.4
  667.3 66.2 reduce-scatter.1
where the time goes:
time: 746 us; the launch traced here: 742 us
  waiting for transfers between devices  306 us (41%)
  blocking collectives  269 us (36%)
  other arithmetic  104 us (14%)
  local copies, waits for them, and re-layouts  36.6 us (5%)
  between operations  13.4 us (2%)
  matrix products  7.92 us (1%)
    all_gather x2, blocking collectives, joined(): everything = jax.tree.map(lambda part: lax.all_gather(part, axis), value)  172 us
    all_gather x1, waiting for transfers between devices, joined(): everything = jax.tree.map(lambda part: lax.all_gather(part, axis), value)  128 us
    all_gather x1, waiting for transfers between devices, body(): stream = lax.all_gather(stream_local, 'seq', axis=2, tiled=True)  123 us
    add x63, other arithmetic, combine(): earlier[2] * left_factor[..., None] + later[2] * right_factor[..., None]  90.8 us
    all_gather x1, blocking collectives, body(): lax.all_gather(hidden, 'seq', axis=1, tiled=True)  74.6 us
    reduce_scatter x1, waiting for transfers between devices, body(): lax.psum_scatter(ffn_part.astype(jnp.bfloat16), 'kvh', scatter_dimension=...  55.2 us
    psum x1, blocking collectives, body(): summed = lax.psum(projected.astype(jnp.bfloat16), 'kvh').astype(jnp.float32)  22.7 us
  transfers between devices with their start and end apart: 3, of which 3 were waited for; matrix products, arithmetic and copies ran while one was open for 2% of the time, Pallas kernels for 0%

commit v1 on v0

v1 whole, which is shorter than its diff:
```python
import functools
import math

import jax
import jax.numpy as jnp
from jax import lax
from jax.experimental import pallas as pl
from jax.experimental.pallas import tpu as pltpu
from jax.sharding import PartitionSpec as P

theta_base = 500000.0
ntk_factor = 4.0
norm_eps = 1e-05
masked_score = -1e30

MESH = pl.DeviceIdType.MESH
NX, NY, NZ, NC = 4, 4, 16, 2
TOK = 128
DH = 128
HEADS = 8
PRE, SUF, NEW = 512, 256, 128
KEYS = PRE + SUF + NEW
QD = 2048
HID = 56
HPAD = 64
BF, F32 = jnp.bfloat16, jnp.float32


def rotary_tables(lengths, prefix_len, head_dim, step_count):
    step_index = jnp.arange(step_count, dtype=jnp.int32)
    position = (prefix_len + lengths[:, None] + step_index[None, :]).astype(jnp.float32)
    anchor = float(prefix_len // 4)
    growth = ntk_factor * (position + 1.0) / anchor - (ntk_factor - 1.0)
    log_base = math.log(theta_base) + head_dim / (head_dim - 2.0) * jnp.log(growth)
    exponent = -2.0 * jnp.arange(head_dim // 2, dtype=jnp.float32) / head_dim
    angles = position[..., None] * jnp.exp(log_base[..., None] * exponent)
    return (jnp.cos(angles), jnp.sin(angles))


def rotate(values, cos_table, sin_table):
    half_dim = values.shape[-1] // 2
    widened = values.astype(jnp.float32)
    first_half = widened[..., :half_dim]
    second = widened[..., half_dim:]
    return jnp.concatenate(
        [first_half * cos_table - second * sin_table, second * cos_table + first_half * sin_table],
        axis=-1,
    ).astype(jnp.bfloat16)


def dev(x, y, z, c):
    return (y * NZ + z, x * NC + c)


def kernel(
    len_ref, q_hbm, new_hbm, pre_hbm, suf_hbm, res_ref, wo_hbm, gain_hbm, wg_hbm, wd_hbm,
    out_ref,
    q_buf, k_buf, v_buf, vt_buf,
    ysend, ystat, yrecv, yrstat,
    zsend, zstat, zrecv, zrstat, att,
    wo_recv, wo_t, rs1_send, rs1_recv, res_recv,
    xt, wg_recv, wg_buf, gain_buf, gsend, grecv,
    ht, wd_recv, wd_t, rs2_send, rs2_recv, str_recv,
    loc, ssem, rsem,
):
    s = lax.axis_index("seq")
    k = lax.axis_index("kvh")
    x, c = k // NC, k % NC
    y, z = s // NZ, s % NZ

    def send(src, dst, stage, to):
        copy = pltpu.make_async_remote_copy(
            src_ref=src, dst_ref=dst, send_sem=ssem.at[stage], recv_sem=rsem.at[stage],
            device_id=to, device_id_type=MESH,
        )
        copy.start()

    def wait(ref, sem):
        pltpu.make_async_copy(ref, ref, sem).wait()

    def zpeer(i):
        return (z + 8 + ((i + 1) // 2) * (1 - 2 * (i % 2))) % NZ

    def plane_peer(i):
        return (x + i // 8) % NX, (y + (i // 2) % NY) % NY, (c + i % 2) % NC

    loads = [
        pltpu.make_async_copy(q_hbm, q_buf, loc.at[0]),
        pltpu.make_async_copy(pre_hbm.at[0], k_buf.at[pl.ds(0, PRE)], loc.at[1]),
        pltpu.make_async_copy(suf_hbm.at[0], k_buf.at[pl.ds(PRE, SUF)], loc.at[2]),
        pltpu.make_async_copy(new_hbm.at[0], k_buf.at[pl.ds(PRE + SUF, NEW)], loc.at[3]),
        pltpu.make_async_copy(pre_hbm.at[1], v_buf.at[pl.ds(0, PRE)], loc.at[4]),
        pltpu.make_async_copy(suf_hbm.at[1], v_buf.at[pl.ds(PRE, SUF)], loc.at[5]),
        pltpu.make_async_copy(new_hbm.at[1], v_buf.at[pl.ds(PRE + SUF, NEW)], loc.at[6]),
    ]
    for copy in loads:
        copy.start()
    own_wg = pltpu.make_async_copy(wg_hbm.at[:, pl.ds(pl.multiple_of(x * QD, QD), QD)], wg_recv.at[x], loc.at[7])
    own_wo = pltpu.make_async_copy(wo_hbm.at[pl.ds(pl.multiple_of(y * 256, 256), 256)], wo_recv.at[y], loc.at[8])
    own_wd = pltpu.make_async_copy(wd_hbm.at[pl.ds(pl.multiple_of(y * 896, 896), 896)], wd_recv.at[y], loc.at[9])
    own_gain = pltpu.make_async_copy(gain_hbm.at[x], gain_buf, loc.at[10])
    for copy in (own_wg, own_wo, own_wd, own_gain):
        copy.start()

    barrier = pltpu.get_barrier_semaphore()

    def greet_z(i, carry):
        pl.semaphore_signal(barrier, inc=1, device_id=dev(x, y, zpeer(i), c), device_id_type=MESH)
        return carry

    def greet_plane(i, carry):
        xp, yp, cp = plane_peer(i)
        pl.semaphore_signal(barrier, inc=1, device_id=dev(xp, yp, z, cp), device_id_type=MESH)
        return carry

    lax.fori_loop(0, NZ - 1, greet_z, 0)
    lax.fori_loop(1, 32, greet_plane, 0)

    for copy in loads:
        copy.wait()
    vt_buf[...] = v_buf[...].T
    length = len_ref[s]
    row = lax.broadcasted_iota(jnp.int32, (SUF + NEW, TOK), 0)
    lane = lax.broadcasted_iota(jnp.int32, (SUF + NEW, TOK), 1)
    live = (lane % 64 == s) & ((row < length) | ((row >= SUF) & (row - SUF <= lane // 64)))
    scale = 1.0 / math.sqrt(DH)

    def attend(dst, stat, yq):
        for h in range(2):
            qt = q_buf[yq * 2 + h]
            raw = jnp.dot(k_buf[...], qt, preferred_element_type=F32) * scale
            first = raw[:PRE]
            second = jnp.where(live, raw[PRE:], masked_score)
            peak = jnp.maximum(
                jnp.max(first, axis=0, keepdims=True), jnp.max(second, axis=0, keepdims=True)
            )
            e1 = jnp.exp(first - peak)
            e2 = jnp.exp(second - peak)
            total = jnp.sum(e1, axis=0, keepdims=True) + jnp.sum(e2, axis=0, keepdims=True)
            acc = jnp.dot(vt_buf[:, :PRE], e1.astype(BF), preferred_element_type=F32)
            acc = acc + jnp.dot(vt_buf[:, PRE:], e2.astype(BF), preferred_element_type=F32)
            dst[pl.ds(h * DH, DH)] = acc.astype(BF)
            stat[pl.ds(2 * h, 1)] = peak
            stat[pl.ds(2 * h + 1, 1)] = total

    def y_hop(d, carry):
        yp = (y + d) % NY
        attend(ysend.at[yp], ystat.at[yp], yp)
        send(ysend.at[yp], yrecv.at[y], 0, dev(x, yp, z, c))
        send(ystat.at[yp], yrstat.at[y], 1, dev(x, yp, z, c))
        return carry

    pl.semaphore_wait(barrier, 46)
    def wg_hop(d, carry):
        xp = (x + d) % NX
        send(wg_hbm.at[:, pl.ds(pl.multiple_of(xp * QD, QD), QD)], wg_recv.at[x], 8, dev(xp, y, z, c))
        return carry

    lax.fori_loop(1, NX, wg_hop, 0)
    @pl.when(x != y)
    def _():
        send(res_ref.at[pl.ds(pl.multiple_of(k * 16, 16), 16)], res_recv, 9, dev(y, x, z, c))

    @pl.when(x == y)
    def _():
        res_recv[...] = res_ref[pl.ds(pl.multiple_of(k * 16, 16), 16)]

    lax.fori_loop(1, NY, y_hop, 0)
    attend(yrecv.at[y], yrstat.at[y], y)
    wait(yrecv.at[pl.ds(0, NY - 1)], rsem.at[0])
    wait(yrstat.at[pl.ds(0, NY - 1)], rsem.at[1])

    for h in range(2):
        peaks = [yrstat[i, pl.ds(2 * h, 1)] for i in range(NY)]
        joint = functools.reduce(jnp.maximum, peaks)
        facs = [jnp.exp(p - joint) for p in peaks]
        total = sum(yrstat[i, pl.ds(2 * h + 1, 1)] * facs[i] for i in range(NY))
        acc = sum(yrecv[i, pl.ds(h * DH, DH)].astype(F32) * facs[i] for i in range(NY))
        zsend[pl.ds(h * 8, 8)] = acc.astype(BF).reshape(8, 16, TOK)
        zstat[h, pl.ds(0, 1)] = joint
        zstat[h, pl.ds(1, 1)] = total

    def z_hop(i, carry):
        zp = zpeer(i)
        send(zsend.at[zp], zrecv.at[z], 2, dev(x, y, zp, c))
        send(zstat.at[zp // 8], zrstat.at[z], 3, dev(x, y, zp, c))
        return carry

    lax.fori_loop(0, NZ - 1, z_hop, 0)

    def wy_hop(d, carry):
        yp = (y + d) % NY
        send(wo_hbm.at[pl.ds(pl.multiple_of(yp * 256, 256), 256)], wo_recv.at[y], 10, dev(x, yp, z, c))
        return carry

    def wd_hop(d, carry):
        yp = (y + d) % NY
        send(wd_hbm.at[pl.ds(pl.multiple_of(yp * 896, 896), 896)], wd_recv.at[y], 11, dev(x, yp, z, c))
        return carry

    lax.fori_loop(1, NY, wy_hop, 0)
    lax.fori_loop(1, NY, wd_hop, 0)
    zrecv[z] = zsend[z]
    zrstat[z] = zstat[z // 8]
    wait(zrecv.at[pl.ds(0, NZ - 1)], rsem.at[2])
    wait(zrstat.at[pl.ds(0, NZ - 1)], rsem.at[3])

    peaks = [zrstat[i, pl.ds(0, 1)] for i in range(NZ)]
    joint = functools.reduce(jnp.maximum, peaks)
    facs = [jnp.exp(p - joint) for p in peaks]
    total = sum(zrstat[i, pl.ds(1, 1)] * facs[i] for i in range(NZ))
    acc = sum(zrecv[i].astype(F32) * facs[i] for i in range(NZ))
    att[z] = (acc / total).astype(BF)

    def a_hop(i, carry):
        send(att.at[z], att.at[z], 4, dev(x, y, zpeer(i), c))
        return carry

    lax.fori_loop(0, NZ - 1, a_hop, 0)

    own_wo.wait()
    wait(wo_recv.at[pl.ds(0, NY - 1)], rsem.at[10])
    for i in range(NY):
        wo_t[pl.ds(i * 128, 128)] = wo_recv[i].T
    own_wg.wait()
    own_gain.wait()
    wait(wg_recv.at[pl.ds(0, NX - 1)], rsem.at[8])

    def scale_gain(i, carry):
        wg_buf[pl.ds(pl.multiple_of(i * 112, 112), 112)] = (wg_recv[i].astype(F32) * gain_buf[...]).astype(BF)
        return carry

    lax.fori_loop(0, NX, scale_gain, 0)
    wait(att.at[pl.ds(0, NZ - 1)], rsem.at[4])

    proj = jnp.dot(wo_t[...], att[...].reshape(256, TOK), preferred_element_type=F32)
    rs1_send[...] = proj.astype(BF).reshape(32, 16, TOK)

    def rs1_hop(i, carry):
        xp, yp, cp = plane_peer(i)
        send(rs1_send.at[xp * 8 + yp * 2 + cp], rs1_recv.at[x * 8 + y * 2 + c], 5, dev(xp, yp, z, cp))
        return carry

    lax.fori_loop(1, 32, rs1_hop, 0)
    me = x * 8 + y * 2 + c
    rs1_recv[me] = rs1_send[me]

    @pl.when(x != y)
    def _():
        wait(res_recv, rsem.at[9])

    wait(rs1_recv.at[pl.ds(0, 31)], rsem.at[5])
    summed = jnp.sum(rs1_recv[...].astype(F32), axis=0)
    xt[z, y, c] = (res_recv[...].astype(F32) + summed).astype(BF)

    def s_hop(i, carry):
        send(xt.at[z, y, c], xt.at[z, y, c], 6, dev(x, y, zpeer(i), c))
        return carry

    lax.fori_loop(0, NZ - 1, s_hop, 0)

    @pl.when(x != y)
    def _():
        send(xt.at[z, y, c], str_recv, 12, dev(y, x, z, c))

    @pl.when(x == y)
    def _():
        str_recv[...] = xt[z, y, c]

    own_wd.wait()
    wait(wd_recv.at[pl.ds(0, NY - 1)], rsem.at[11])

    def down_block(i, carry):
        zero = jnp.zeros((HPAD - HID, 128), BF)
        tall = [
            jnp.concatenate([wd_recv[i, pl.ds(n * HID, HID)], zero], axis=0) for n in range(NZ)
        ]
        for n in range(NZ // 2):
            both = jnp.concatenate([tall[2 * n], tall[2 * n + 1]], axis=0)
            wd_t[pl.ds(pl.multiple_of(i * 128, 128), 128), pl.ds(n * 128, 128)] = both.T
        return carry

    lax.fori_loop(0, NY, down_block, 0)
    wait(xt.at[pl.ds(0, NZ - 1), 0, 0], rsem.at[6])

    def s2_hop(i, carry):
        yp, cp = (y + i // 2) % NY, (c + i % 2) % NC
        send(xt.at[:, y, c], xt.at[:, y, c], 7, dev(x, yp, z, cp))
        return carry

    lax.fori_loop(1, 8, s2_hop, 0)
    wait(xt.at[pl.ds(0, 14)], rsem.at[7])

    stream = xt[...].reshape(QD, TOK)
    wide = stream.astype(F32)
    squares = jnp.sum(wide * wide, axis=0, keepdims=True)
    part = jnp.dot(wg_buf[...], stream, preferred_element_type=F32)
    for i in range(NX):
        gsend[i, pl.ds(0, 112)] = part[i * 112 : (i + 1) * 112]
        gsend[i, pl.ds(112, 8)] = jnp.broadcast_to(squares, (8, TOK))

    def g_hop(d, carry):
        xp = (x + d) % NX
        send(gsend.at[xp], grecv.at[x], 13, dev(xp, y, z, c))
        return carry

    lax.fori_loop(1, NX, g_hop, 0)
    grecv[x] = gsend[x]
    wait(grecv.at[pl.ds(0, NX - 1)], rsem.at[13])
    gu = jnp.sum(grecv[...], axis=0)
    inv_rms = lax.rsqrt(gu[112:113] * (1.0 / (NX * QD)) + norm_eps)
    gate = gu[:HID] * inv_rms
    up = gu[HID : 2 * HID] * inv_rms
    hidden = gate / (1.0 + jnp.exp(-gate)) * up
    ht[z] = jnp.concatenate([hidden, jnp.zeros((HPAD - HID, TOK), F32)], axis=0).astype(BF)

    def h_hop(i, carry):
        send(ht.at[z], ht.at[z], 14, dev(x, y, zpeer(i), c))
        return carry

    lax.fori_loop(0, NZ - 1, h_hop, 0)
    wait(ht.at[pl.ds(0, NZ - 1)], rsem.at[14])

    down = jnp.dot(wd_t[...], ht[...].reshape(NZ * HPAD, TOK), preferred_element_type=F32)
    rs2_send[...] = down.astype(BF).reshape(32, 16, TOK)

    def rs2_hop(i, carry):
        xp, yp, cp = plane_peer(i)
        send(rs2_send.at[yp * 8 + xp * 2 + cp], rs2_recv.at[me], 15, dev(xp, yp, z, cp))
        return carry

    lax.fori_loop(1, 32, rs2_hop, 0)
    rs2_recv[me] = rs2_send[y * 8 + x * 2 + c]

    @pl.when(x != y)
    def _():
        wait(str_recv, rsem.at[12])

    wait(rs2_recv.at[pl.ds(0, 31)], rsem.at[15])
    result = str_recv[...].astype(F32) + jnp.sum(rs2_recv[...].astype(F32), axis=0)
    rounded = result.astype(BF)
    out_ref[0] = rounded[:, :64]
    out_ref[1] = rounded[:, 64:]

    wait(ysend.at[pl.ds(0, 3)], ssem.at[0])
    wait(ystat.at[pl.ds(0, 3)], ssem.at[1])
    wait(zsend.at[pl.ds(0, 15)], ssem.at[2])
    wait(zrstat.at[pl.ds(0, 15)], ssem.at[3])
    wait(att.at[pl.ds(0, 15)], ssem.at[4])
    wait(rs1_send.at[pl.ds(0, 31)], ssem.at[5])
    wait(xt.at[pl.ds(0, NZ - 1), 0, 0], ssem.at[6])
    wait(xt.at[pl.ds(0, 14)], ssem.at[7])
    wait(wg_recv.at[pl.ds(0, 3)], ssem.at[8])
    wait(wo_recv.at[pl.ds(0, 3)], ssem.at[10])
    wait(wd_recv.at[pl.ds(0, 3)], ssem.at[11])
    wait(gsend.at[pl.ds(0, 3)], ssem.at[13])
    wait(ht.at[pl.ds(0, 15)], ssem.at[14])
    wait(rs2_send.at[pl.ds(0, 31)], ssem.at[15])

    @pl.when(x != y)
    def _():
        wait(res_recv, ssem.at[9])
        wait(str_recv, ssem.at[12])


def body(
    resid,
    queries,
    new_kv,
    prefix_cache,
    suffix_cache,
    suffix_lengths,
    out_weight,
    norm_gain,
    gate_up,
    down_weight,
):
    seq_index = lax.axis_index("seq")
    requests, step_count, local_heads, head_dim = queries.shape
    prefix_len = prefix_cache.shape[1] * lax.axis_size("seq")
    cos_table, sin_table = rotary_tables(suffix_lengths, prefix_len, head_dim, step_count)
    rotated = rotate(queries, cos_table[:, :, None, :], sin_table[:, :, None, :])
    q_t = rotated.transpose(2, 3, 1, 0).reshape(local_heads, head_dim, TOK)
    own_cos = lax.dynamic_slice_in_dim(cos_table, seq_index, 1, 0)[0]
    own_sin = lax.dynamic_slice_in_dim(sin_table, seq_index, 1, 0)[0]
    new_keys = rotate(new_kv[0, 0, :, 0], own_cos, own_sin)
    fresh = jnp.stack([new_keys, new_kv[1, 0, :, 0]])
    fresh = jnp.pad(fresh, ((0, 0), (0, NEW - step_count), (0, 0)))
    resid_t = resid.transpose(2, 1, 0).reshape(128, TOK)
    wg = gate_up[:, :, 0, :].transpose(0, 2, 1).reshape(2 * HID, 4 * QD)
    any_spec = pl.BlockSpec(memory_space=pl.ANY)
    vmem = pltpu.VMEM
    result = pl.pallas_call(
        kernel,
        out_shape=jax.ShapeDtypeStruct((2, 16, 64), BF),
        in_specs=[pl.BlockSpec(memory_space=pltpu.SMEM)] + [any_spec] * 4
        + [pl.BlockSpec(memory_space=pltpu.VMEM)] + [any_spec] * 4,
        out_specs=pl.BlockSpec(memory_space=pltpu.VMEM),
        scratch_shapes=[
            vmem((HEADS, DH, TOK), BF), vmem((KEYS, DH), BF), vmem((KEYS, DH), BF), vmem((DH, KEYS), BF),
            vmem((NY, 256, TOK), BF), vmem((NY, 8, TOK), F32), vmem((NY, 256, TOK), BF), vmem((NY, 8, TOK), F32),
            vmem((NZ, 16, TOK), BF), vmem((2, 2, TOK), F32), vmem((NZ, 16, TOK), BF), vmem((NZ, 2, TOK), F32),
            vmem((NZ, 16, TOK), BF),
            vmem((NY, 256, 128), BF), vmem((512, 256), BF), vmem((32, 16, TOK), BF), vmem((32, 16, TOK), BF),
            vmem((16, TOK), BF),
            vmem((NZ, NY, NC, 16, TOK), BF), vmem((NX, 112, QD), BF), vmem((NX * 112, QD), BF), vmem((1, QD), F32),
            vmem((NX, 120, TOK), F32), vmem((NX, 120, TOK), F32),
            vmem((NZ, HPAD, TOK), BF), vmem((NY, 896, 128), BF), vmem((512, NZ * HPAD), BF),
            vmem((32, 16, TOK), BF), vmem((32, 16, TOK), BF), vmem((16, TOK), BF),
            pltpu.SemaphoreType.DMA((11,)), pltpu.SemaphoreType.DMA((16,)), pltpu.SemaphoreType.DMA((16,)),
        ],
        compiler_params=pltpu.CompilerParams(
            collective_id=0, has_side_effects=True, vmem_limit_bytes=40 * 1024 * 1024
        ),
        name="layer",
    )(
        suffix_lengths, q_t, fresh, prefix_cache[:, :, 0, :], suffix_cache[:, 0, :, 0, :], resid_t,
        out_weight, norm_gain.reshape(4, 1, QD), wg, down_weight,
    )
    return result.transpose(2, 0, 1)


def solution(mesh):
    placed = (
        P(None, None, "seq"),
        P(None, None, "kvh", None),
        P(None, "seq", None, "kvh", None),
        P(None, "seq", "kvh", None),
        P(None, "seq", None, "kvh", None),
        P(),
        P("kvh", "seq"),
        P(),
        P(None, None, "kvh", "seq"),
        P("kvh", "seq"),
    )
    return jax.shard_map(
        body, mesh=mesh, in_specs=placed, out_specs=P(None, None, ("seq", "kvh")), check_vma=False
    )
```

time: 746 us -> 96.7 us (0.13)
  waiting for transfers between devices: 306 us -> 0 us
  blocking collectives: 269 us -> 0 us
  other arithmetic: 104 us -> 3.47 us
  Pallas kernels: 0 us -> 87.8 us
  local copies, waits for them, and re-layouts: 36.6 us -> 4.9 us
  between operations: 13.4 us -> 0.19 us
  matrix products: 7.92 us -> 0 us
    all_gather x2 -> x0, waiting for transfers between devices: 251 us -> none  [the longest x1 128 us: joined(): everything = jax.tree.map(lambda part: lax.all_gather(part, axis), value)]
    all_gather x3 -> x0, blocking collectives: 247 us -> none  [the longest x2 172 us: joined(): everything = jax.tree.map(lambda part: lax.all_gather(part, axis), value)]
    add x63 -> x0, other arithmetic: 90.8 us -> none  [combine(): earlier[2] * left_factor[..., None] + later[2] * right_factor[..., None]]
    pallas_call x0 -> x1, Pallas kernels: none -> 87.8 us  [body(): pl.pallas_call(kernel, out_shape=jax.ShapeDtypeStruct((2, 16, 64), BF), i...]
    reduce_scatter x1 -> x0, waiting for transfers between devices: 55.2 us -> none  [body(): lax.psum_scatter(ffn_part.astype(jnp.bfloat16), 'kvh', scatter_dimension=...]
    psum x1 -> x0, blocking collectives: 22.7 us -> none  [body(): summed = lax.psum(projected.astype(jnp.bfloat16), 'kvh').astype(jnp.float32)]
    convert_element_type x6 -> x0, local copies, waits for them, and re-layouts: 18.1 us -> none  [the longest x2 10.2 us: body(): stream.reshape(requests * step_count, model_width).astype(jnp.float32)]
    mul x126 -> x0, local copies, waits for them, and re-layouts: 12.9 us -> none  [the longest x63 6.6 us: combine(): later[2] * right_factor[..., None]]
  transfers between devices with their start and end apart: 3 -> 0, of which waited for: 3 -> 0; matrix products, arithmetic and copies ran while one was open for 2% -> 0% of each run, Pallas kernels for 0% -> 0%
where the time goes in v1:
time: 96.7 us; the launch traced here: 96.4 us
  Pallas kernels  87.8 us (91%)
  local copies, waits for them, and re-layouts  4.9 us (5%)
  other arithmetic  3.47 us (4%)
    pallas_call x1, Pallas kernels, body(): pl.pallas_call(kernel, out_shape=jax.ShapeDtypeStruct((2, 16, 64), BF), i...  87.8 us
    unnamed x22, local copies, waits for them, and re-layouts  2.22 us

profile of v1, /device:TPU:1, one launch (start us, length us, event | category | flops | bytes accessed | tf_op | source)
XLA Modules:
  0.0 96.4 jit_solution(14073320037119596912)
XLA Ops:
  0.0 0.0 copy-start.9
  0.0 1.0 %copy_convert_fusion = f32[64,2,8,128]{3,0,1,2:T(8,128)S(1)} fusion(bf16[64,2,8,128]{3,2,1,0:T(8,128)(2,1)} %param.11), kind=kLoop, calls=%fused_computation.3 | loop fusion | flops 131072 | bytes 786432 | tf_op jit(solution)/shard_map/convert_element_type | solution.py:42
  1.0 0.0 copy-start.8
  1.0 0.0 copy-start
  1.1 0.0 copy-start.1
  1.1 0.0 copy-start.2
  1.1 0.0 copy-start.4
  1.1 0.0 copy-start.5
  1.1 0.0 copy-start.6
  1.1 0.8 broadcast_add_fusion
  2.0 0.3 fusion.6
  2.3 0.0 copy-start.7
  2.3 0.3 subtract_convert_fusion
  2.6 0.9 pad_maximum_fusion
  3.4 0.0 copy-done.7
  3.4 1.1 %copy.21.q_hbm = bf16[8,128,128]{2,1,0:T(8,128)(2,1)S(1)} copy(bf16[8,128,128]{1,2,0:T(8,128)(2,1)} %bitcast.31) | data formatting | bytes 524288 | tf_op jit(solution)/shard_map/reshape | solution.py:383
  4.6 0.0 copy-done.9
  4.6 0.7 constant_dynamic-slice_fusion
  5.3 0.1 fusion.7
  5.4 0.1 fusion.4.new_hbm
  5.5 0.0 copy-done.8
  5.5 0.6 copy.20
  6.1 0.9 copy.22.res_ref
  6.9 0.0 copy-done
  7.0 0.0 copy-done.1
  7.0 0.0 copy-done.2
  7.0 0.0 copy-done.4
  7.0 0.0 copy-done.5
  7.0 0.0 copy-done.6
  7.0 0.0 copy-start.3
  7.0 0.9 copy-done.3
  8.0 87.8 %layer.1 = bf16[2,16,64]{2,1,0:T(8,128)(2,1)S(1)} custom-call(s32[64]{0:T(128)S(1)} %copy-done.6, bf16[8,128,128]{2,1,0:T(8,128)(2,1)S(1)} %copy.21.q_hbm, bf16[2,128,128]{2,1,0:T(8,128)(2,1)S(1)} %fusion.4.new_hbm, bf16[2,512,128]{2,1,0:T(8,128)(2,1)S(1)} %bitcast.27, bf16[2,256,128]{2,1,0:T(8,128)(2,1)S(1)} %bitcast.28, ...), custom_call_target="tpu_custom_call" | custom-call | tf_op jit(solution)/shard_map/layer/pallas_call | solution.py:393
  95.8 0.6 copy.25
  (4 shorter events, 0.0 us)
Async XLA Ops:
  0.0 4.6 %copy-start.9 = (bf16[2,1,2,1,128]{4,2,3,1,0:T(2,128)(2,1)S(1)}, bf16[2,1,2,1,128]{4,2,3,1,0:T(2,128)(2,1)}, u32[]{:S(2)}) copy-start(bf16[2,1,2,1,128]{4,2,3,1,0:T(2,128)(2,1)} %param.12) | copy-start | bytes 3076
  1.0 4.4 %copy-start.8 = (bf16[64,2,128]{2,1,0:T(2,128)(2,1)S(1)}, bf16[64,2,128]{2,1,0:T(2,128)(2,1)}, u32[]{:S(2)}) copy-start(bf16[64,2,128]{2,1,0:T(2,128)(2,1)} %param.10) | copy-start | bytes 98308
  1.0 5.9 %copy-start = (bf16[2,8192,1,56]{1,3,2,0:T(8,128)(2,1)S(1)}, bf16[2,8192,1,56]{1,3,2,0:T(8,128)(2,1)}, u32[]{:S(2)}) copy-start(bf16[2,8192,1,56]{1,3,2,0:T(8,128)(2,1)} %param.18) | copy-start | bytes 5505028
  1.1 5.9 %copy-start.1 = (bf16[3584,128]{1,0:T(8,128)(2,1)S(1)}, bf16[3584,128]{1,0:T(8,128)(2,1)}, u32[]{:S(2)}) copy-start(bf16[3584,128]{1,0:T(8,128)(2,1)} %wd_hbm.1) | copy-start | bytes 2752516
  1.1 5.9 %copy-start.2 = (bf16[2,512,1,128]{3,1,2,0:T(8,128)(2,1)S(1)}, bf16[2,512,1,128]{3,1,2,0:T(8,128)(2,1)}, u32[]{:S(2)}) copy-start(bf16[2,512,1,128]{3,1,2,0:T(8,128)(2,1)} %param.13) | copy-start | bytes 786436
  1.1 5.9 %copy-start.4 = (bf16[2,1,256,1,128]{4,2,3,1,0:T(8,128)(2,1)S(1)}, bf16[2,1,256,1,128]{4,2,3,1,0:T(8,128)(2,1)}, u32[]{:S(2)}) copy-start(bf16[2,1,256,1,128]{4,2,3,1,0:T(8,128)(2,1)} %param.14) | copy-start | bytes 393220
  1.1 5.9 %copy-start.5 = (f32[8192]{0:T(1024)S(1)}, f32[8192]{0:T(1024)}, u32[]{:S(2)}) copy-start(f32[8192]{0:T(1024)} %param.17) | copy-start | bytes 98308
  1.1 5.9 %copy-start.6 = (s32[64]{0:T(128)S(1)}, s32[64]{0:T(128)}, u32[]{:S(2)}) copy-start(s32[64]{0:T(128)} %len_ref.1) | copy-start | bytes 772
  2.3 1.1 %copy-start.7 = (f32[64,2,64]{2,0,1:T(8,128)}, f32[64,2,64]{2,0,1:T(8,128)S(1)}, u32[]{:S(2)}) copy-start(f32[64,2,64]{2,0,1:T(8,128)S(1)} %get-tuple-element.10) | copy-start | bytes 98308
  7.0 1.0 copy-start.3

commit v2 on v1

v2 whole, which is shorter than its diff:
```python
import math

import jax
import jax.numpy as jnp
from jax import lax
from jax.experimental import pallas as pl
from jax.experimental.pallas import tpu as pltpu
from jax.sharding import PartitionSpec as P

theta_base = 500000.0
ntk_factor = 4.0
norm_eps = 1e-05
masked_score = -1e30

MESH = pl.DeviceIdType.MESH
NX, NY, NZ, NC = 4, 4, 16, 2
REQ = 64
TOK = 128
DH = 128
HEADS = 8
PRE, SUF, NEW = 512, 256, 128
KEYS = PRE + SUF + NEW
PREFIX = PRE * NY * NZ
ED = 1024
HID = 56
HPAD = 64
BF, F32 = jnp.bfloat16, jnp.float32
TN = (((0,), (0,)), ((), ()))


def rotary(position, index):
    growth = ntk_factor * (position + 1.0) / float(PREFIX // 4) - (ntk_factor - 1.0)
    log_base = math.log(theta_base) + DH / (DH - 2.0) * jnp.log(growth)
    angles = position * jnp.exp(log_base * (-2.0 * index.astype(F32) / DH))
    return jnp.cos(angles), jnp.sin(angles)


def dev(x, y, z, c):
    return (y * NZ + z, x * NC + c)


def kernel(
    lens_hbm, new_hbm, res_hbm, q_hbm, pre_hbm, suf_hbm, wo_hbm, gain_hbm, wg_hbm, wd_hbm,
    out_ref,
    lens_ref, new_ref, res_ref, q_raw, q_wide, q_buf, k_buf, v_buf, vt_buf, new_buf, res_t,
    ysend, ystat, yrecv, yrstat,
    zsend, zstat, zrecv, zrstat, att,
    wo_recv, wo_t, rs1_send, rs1_recv, res_recv,
    xt, wg_recv, wg_buf, gain_buf, gsend, grecv,
    ht, wd_recv, wd_t, rs2_send, rs2_recv, str_recv,
    loc, ssem, rsem,
):
    s = lax.axis_index("seq")
    k = lax.axis_index("kvh")
    x, c = k // NC, k % NC
    y, z = s // NZ, s % NZ
    zc, zi = z // 8, z % 8
    owner = c == zc

    def send(src, dst, stage, to):
        copy = pltpu.make_async_remote_copy(
            src_ref=src, dst_ref=dst, send_sem=ssem.at[stage], recv_sem=rsem.at[stage],
            device_id=to, device_id_type=MESH,
        )
        copy.start()

    def wait(ref, sem):
        pltpu.make_async_copy(ref, ref, sem).wait()

    def zpeer(i):
        return (z + 8 + ((i + 1) // 2) * (1 - 2 * (i % 2))) % NZ

    def plane_peer(i):
        return (x + i // 8) % NX, (y + (i // 2) % NY) % NY, (c + i % 2) % NC

    load_q = pltpu.make_async_copy(q_hbm, q_raw, loc.at[0])
    load_q.start()
    smalls = [
        pltpu.make_async_copy(lens_hbm, lens_ref, loc.at[9]),
        pltpu.make_async_copy(new_hbm, new_ref, loc.at[10]),
        pltpu.make_async_copy(res_hbm, res_ref, loc.at[11]),
    ]
    for copy in smalls:
        copy.start()
    loads = [
        pltpu.make_async_copy(pre_hbm.at[0], k_buf.at[pl.ds(0, PRE)], loc.at[1]),
        pltpu.make_async_copy(suf_hbm.at[0], k_buf.at[pl.ds(PRE, SUF)], loc.at[2]),
        pltpu.make_async_copy(pre_hbm.at[1], v_buf.at[pl.ds(0, PRE)], loc.at[3]),
        pltpu.make_async_copy(suf_hbm.at[1], v_buf.at[pl.ds(PRE, SUF)], loc.at[4]),
    ]
    for copy in loads:
        copy.start()

    barrier = pltpu.get_barrier_semaphore()

    def greet_z(i, carry):
        pl.semaphore_signal(barrier, inc=1, device_id=dev(x, y, zpeer(i), c), device_id_type=MESH)
        return carry

    def greet_plane(i, carry):
        xp, yp, cp = plane_peer(i)
        pl.semaphore_signal(barrier, inc=1, device_id=dev(xp, yp, z, cp), device_id_type=MESH)
        return carry

    lax.fori_loop(0, NZ - 1, greet_z, 0)
    lax.fori_loop(1, 32, greet_plane, 0)
    own_wg = pltpu.make_async_copy(wg_hbm.at[:, pl.ds(pl.multiple_of(k * ED, ED), ED)], wg_recv.at[k], loc.at[5])
    own_wo = pltpu.make_async_copy(wo_hbm.at[pl.ds(pl.multiple_of(y * 256, 256), 256)], wo_recv.at[y], loc.at[6])
    own_wd = pltpu.make_async_copy(wd_hbm.at[pl.ds(pl.multiple_of(y * 896, 896), 896)], wd_recv.at[y], loc.at[7])
    own_gain = pltpu.make_async_copy(gain_hbm.at[k], gain_buf, loc.at[8])
    for copy in (own_wg, own_wo, own_wd, own_gain):
        copy.start()

    for copy in smalls:
        copy.wait()
    lens = lens_ref[...]
    position = (PREFIX + jnp.concatenate([lens, lens + 1], axis=1)).astype(F32)
    cos, sin = rotary(position, lax.broadcasted_iota(jnp.int32, (DH // 2, TOK), 0))
    token = lax.broadcasted_iota(jnp.int32, (TOK, TOK), 0)
    place = lax.broadcasted_iota(jnp.int32, (TOK, TOK), 1)
    perm = (token == 2 * (place % REQ) + place // REQ).astype(F32).astype(BF)
    load_q.wait()
    q_wide[...] = q_raw[...].astype(F32).reshape(TOK * HEADS, DH)
    for h in range(HEADS):
        rows = q_wide[pl.ds(h, TOK, stride=HEADS)].astype(BF)
        turned = lax.dot_general(rows, perm, TN, preferred_element_type=F32)
        a, b = turned[: DH // 2], turned[DH // 2 :]
        q_buf[h // 2, :, pl.ds((h % 2) * TOK, TOK)] = jnp.concatenate(
            [a * cos - b * sin, b * cos + a * sin], axis=0
        ).astype(BF)

    own = lax.broadcasted_iota(jnp.int32, (1, REQ), 1) == s
    length = jnp.sum(jnp.where(own, lens.astype(F32), 0.0), axis=1, keepdims=True)
    lane8 = lax.broadcasted_iota(jnp.int32, (8, DH), 1)
    row8 = lax.broadcasted_iota(jnp.int32, (8, DH), 0)
    cos8, sin8 = rotary(PREFIX + length + row8.astype(F32), lane8 % (DH // 2))
    new_buf[...] = jnp.zeros_like(new_buf)
    new_buf[0, pl.ds(0, 2)] = new_ref[0].astype(F32)
    new_buf[1, pl.ds(0, 2)] = new_ref[1].astype(F32)
    fresh = new_buf[0]
    other = pltpu.roll(fresh, DH // 2, 1)
    fresh = fresh * cos8 + jnp.where(lane8 < DH // 2, -other, other) * sin8
    none = jnp.zeros((NEW - 8, DH), F32)
    k_buf[pl.ds(PRE + SUF, NEW)] = jnp.concatenate([fresh, none], axis=0).astype(BF)
    v_buf[pl.ds(PRE + SUF, NEW)] = jnp.concatenate([new_buf[1], none], axis=0).astype(BF)
    for copy in loads:
        copy.wait()
    vt_buf[...] = v_buf[...].T
    row = lax.broadcasted_iota(jnp.int32, (SUF + NEW, 2 * TOK), 0)
    lane = lax.broadcasted_iota(jnp.int32, (SUF + NEW, 2 * TOK), 1)
    live = (lane % REQ == s) & ((row.astype(F32) < length) | ((row >= SUF) & (row - SUF <= (lane // REQ) % 2)))
    scale = 1.0 / math.sqrt(DH)

    def attend(dst, stat, yq):
        raw = jnp.dot(k_buf[...], q_buf[yq], preferred_element_type=F32) * scale
        first = raw[:PRE]
        second = jnp.where(live, raw[PRE:], masked_score)
        peak = jnp.maximum(
            jnp.max(first, axis=0, keepdims=True), jnp.max(second, axis=0, keepdims=True)
        )
        e1 = jnp.exp(first - peak)
        e2 = jnp.exp(second - peak)
        total = jnp.sum(e1, axis=0, keepdims=True) + jnp.sum(e2, axis=0, keepdims=True)
        acc = jnp.dot(vt_buf[:, :PRE], e1.astype(BF), preferred_element_type=F32)
        acc = acc + jnp.dot(vt_buf[:, PRE:], e2.astype(BF), preferred_element_type=F32)
        for h in range(2):
            dst[pl.ds(h * DH, DH)] = acc[:, h * TOK : (h + 1) * TOK].astype(BF)
            stat[pl.ds(2 * h, 1)] = peak[:, h * TOK : (h + 1) * TOK]
            stat[pl.ds(2 * h + 1, 1)] = total[:, h * TOK : (h + 1) * TOK]

    def y_send(yp):
        send(ysend.at[yp], yrecv.at[y], 0, dev(x, yp, z, c))
        send(ystat.at[yp], yrstat.at[y], 1, dev(x, yp, z, c))

    first_y = (y + 2) % NY
    attend(ysend.at[first_y], ystat.at[first_y], first_y)
    pl.semaphore_wait(barrier, 46)
    y_send(first_y)

    def wg_hop(d, carry):
        kp = (k + d) % (NX * NC)
        send(wg_hbm.at[:, pl.ds(pl.multiple_of(kp * ED, ED), ED)], wg_recv.at[k], 8, dev(kp // NC, y, z, kp % NC))
        return carry

    lax.fori_loop(1, NX * NC, wg_hop, 0)

    def y_hop(d, carry):
        yp = (y + 2 * d - 1) % NY
        attend(ysend.at[yp], ystat.at[yp], yp)
        y_send(yp)
        return carry

    lax.fori_loop(1, 3, y_hop, 0)

    res_t[...] = lax.dot_general(res_ref[...], perm, TN, preferred_element_type=F32).astype(BF)

    @pl.when(owner & (x != y))
    def _():
        send(res_t.at[pl.ds(pl.multiple_of(x * 32, 32), 32)], res_recv, 9, dev(y, x, z, c))

    @pl.when(owner & (x == y))
    def _():
        res_recv[...] = res_t[pl.ds(pl.multiple_of(x * 32, 32), 32)]

    attend(yrecv.at[y], yrstat.at[y], y)
    wait(yrecv.at[pl.ds(0, NY - 1)], rsem.at[0])
    wait(yrstat.at[pl.ds(0, NY - 1)], rsem.at[1])

    for h in range(2):
        peaks = [yrstat[i, pl.ds(2 * h, 1)] for i in range(NY)]
        joint = jnp.maximum(jnp.maximum(peaks[0], peaks[1]), jnp.maximum(peaks[2], peaks[3]))
        facs = [jnp.exp(p - joint) for p in peaks]
        total = sum(yrstat[i, pl.ds(2 * h + 1, 1)] * facs[i] for i in range(NY))
        acc = sum(yrecv[i, pl.ds(h * DH, DH)].astype(F32) * facs[i] for i in range(NY))
        zsend[pl.ds(h * 8, 8)] = acc.astype(BF).reshape(8, 16, TOK)
        zstat[h, pl.ds(0, 1)] = joint
        zstat[h, pl.ds(1, 1)] = total

    def z_hop(i, carry):
        zp = zpeer(i)
        send(zstat.at[zp // 8], zrstat.at[z], 3, dev(x, y, zp, c))
        send(zsend.at[zp], zrecv.at[z], 2, dev(x, y, zp, c))
        return carry

    lax.fori_loop(0, NZ - 1, z_hop, 0)

    def wo_hop(d, carry):
        yp = (y + d) % NY
        send(wo_hbm.at[pl.ds(pl.multiple_of(yp * 256, 256), 256)], wo_recv.at[y], 10, dev(x, yp, z, c))
        return carry

    def wd_hop(d, carry):
        yp = (y + d) % NY
        send(wd_hbm.at[pl.ds(pl.multiple_of(yp * 896, 896), 896)], wd_recv.at[y], 11, dev(x, yp, z, c))
        return carry

    lax.fori_loop(1, NY, wo_hop, 0)
    lax.fori_loop(1, NY, wd_hop, 0)
    zrecv[z] = zsend[z]
    zrstat[z] = zstat[z // 8]
    wait(zrstat.at[pl.ds(0, NZ - 1)], rsem.at[3])
    wait(zrecv.at[pl.ds(0, NZ - 1)], rsem.at[2])

    peaks = [zrstat[i, pl.ds(0, 1)] for i in range(NZ)]
    joint = peaks[0]
    for p in peaks[1:]:
        joint = jnp.maximum(joint, p)
    facs = [jnp.exp(p - joint) for p in peaks]
    total = sum(zrstat[i, pl.ds(1, 1)] * facs[i] for i in range(NZ))
    acc = sum(zrecv[i].astype(F32) * facs[i] for i in range(NZ))
    att[z] = (acc / total).astype(BF)

    def a_hop(i, carry):
        send(att.at[z], att.at[z], 4, dev(x, y, zpeer(i), c))
        return carry

    lax.fori_loop(0, NZ - 1, a_hop, 0)

    own_wo.wait()
    wait(wo_recv.at[pl.ds(0, NY - 1)], rsem.at[10])
    for i in range(NY):
        wo_t[pl.ds(i * 128, 128)] = wo_recv[i].T
    wait(att.at[pl.ds(0, NZ - 1)], rsem.at[4])

    proj = jnp.dot(wo_t[...], att[...].reshape(256, TOK), preferred_element_type=F32)
    rs1_send[...] = proj.astype(BF).reshape(16, 32, TOK)
    me = x * 8 + y * 2 + c

    def rs1_hop(i, carry):
        xp, yp = (x + i // 4) % NX, (y + i % 4) % NY
        send(rs1_send.at[xp * 4 + yp], rs1_recv.at[me], 5, dev(xp, yp, z, zc))
        return carry

    lax.fori_loop(1, 16, rs1_hop, 0)

    @pl.when(jnp.logical_not(owner))
    def _():
        send(rs1_send.at[x * 4 + y], rs1_recv.at[me], 5, dev(x, y, z, zc))

    @pl.when(owner & (x != y))
    def _():
        wait(res_recv, rsem.at[9])

    @pl.when(owner)
    def _():
        rs1_recv[me] = rs1_send[x * 4 + y]
        wait(rs1_recv.at[pl.ds(0, 31)], rsem.at[5])
        summed = jnp.sum(rs1_recv[...].astype(F32), axis=0)
        xt[zi, y] = (res_recv[...].astype(F32) + summed).astype(BF)

        def s_hop(i, carry):
            send(xt.at[zi, y], xt.at[zi, y], 6, dev(x, y, zpeer(i), c))
            return carry

        lax.fori_loop(0, NZ - 1, s_hop, 0)
        for cp in range(NC):
            chunk = xt.at[zi, y, pl.ds(cp * 16, 16)]

            @pl.when((x != y) | (c != cp))
            def _():
                send(chunk, str_recv, 12, dev(y, x, z, cp))

            @pl.when((x == y) & (c == cp))
            def _():
                str_recv[...] = chunk[...]

    own_wg.wait()
    own_gain.wait()
    wait(wg_recv.at[pl.ds(0, 7)], rsem.at[8])

    def scale_gain(i, carry):
        wg_buf[pl.ds(pl.multiple_of(i * 112, 112), 112)] = (wg_recv[i].astype(F32) * gain_buf[...]).astype(BF)
        return carry

    lax.fori_loop(0, NX * NC, scale_gain, 0)

    @pl.when(owner)
    def _():
        wait(xt.at[pl.ds(0, 7), 0], rsem.at[6])

    @pl.when(jnp.logical_not(owner))
    def _():
        wait(xt.at[pl.ds(0, 8), 0], rsem.at[6])


    def s2_hop(d, carry):
        send(xt.at[:, y], xt.at[:, y], 7, dev(x, (y + d) % NY, z, c))
        return carry

    lax.fori_loop(1, NY, s2_hop, 0)
    wait(xt.at[:, pl.ds(0, 3)], rsem.at[7])

    stream = xt[...].reshape(ED, TOK)
    part = jnp.dot(wg_buf[...], stream, preferred_element_type=F32)
    gsend[:, pl.ds(0, 112)] = part.astype(BF).reshape(8, 112, TOK)
    wide = stream.astype(F32)
    squares = jnp.sum(wide * wide, axis=0, keepdims=True)
    high = squares.astype(BF).astype(F32)
    row16 = lax.broadcasted_iota(jnp.int32, (16, TOK), 0)
    both = jnp.where(row16 == 0, high, jnp.where(row16 == 1, squares - high, 0.0)).astype(BF)
    for i in range(8):
        gsend[i, pl.ds(112, 16)] = both

    def g_hop(d, carry):
        kp = (k + d) % (NX * NC)
        send(gsend.at[kp], grecv.at[k], 13, dev(kp // NC, y, z, kp % NC))
        return carry

    lax.fori_loop(1, NX * NC, g_hop, 0)
    grecv[k] = gsend[k]

    own_wd.wait()
    wait(wd_recv.at[pl.ds(0, NY - 1)], rsem.at[11])

    def down_block(i, carry):
        zero = jnp.zeros((HPAD - HID, 128), BF)
        tall = [
            jnp.concatenate([wd_recv[i, pl.ds(n * HID, HID)], zero], axis=0) for n in range(NZ)
        ]
        for n in range(NZ // 2):
            pair = jnp.concatenate([tall[2 * n], tall[2 * n + 1]], axis=0)
            wd_t[pl.ds(pl.multiple_of(i * 128, 128), 128), pl.ds(n * 128, 128)] = pair.T
        return carry

    lax.fori_loop(0, NY, down_block, 0)
    wait(grecv.at[pl.ds(0, 7)], rsem.at[13])
    gu = jnp.sum(grecv[...].astype(F32), axis=0)
    inv_rms = lax.rsqrt((gu[112:113] + gu[113:114]) * (1.0 / (8 * ED)) + norm_eps)
    gate = gu[:HID] * inv_rms
    up = gu[HID : 2 * HID] * inv_rms
    hidden = gate / (1.0 + jnp.exp(-gate)) * up
    ht[z] = jnp.concatenate([hidden, jnp.zeros((HPAD - HID, TOK), F32)], axis=0).astype(BF)

    def zd(d):
        return (z + d + NZ) % NZ

    def h_send(block, d, stage):
        send(ht.at[block], ht.at[block], stage, dev(x, y, zd(d), c))

    h_send(z, 5, 16)
    h_send(z, -5, 17)
    h_send(z, 8, 14)
    h_send(z, 2, 18)
    h_send(z, -2, 19)
    h_send(z, 1, 14)
    h_send(z, -1, 14)
    wait(ht.at[0], rsem.at[18])
    h_send(zd(-2), 1, 14)
    wait(ht.at[0], rsem.at[19])
    h_send(zd(2), -1, 14)
    wait(ht.at[0], rsem.at[16])
    h_send(zd(-5), 2, 14)
    h_send(zd(-5), 1, 14)
    h_send(zd(-5), -1, 14)
    wait(ht.at[0], rsem.at[17])
    h_send(zd(5), -2, 14)
    h_send(zd(5), -1, 14)
    h_send(zd(5), 1, 14)
    wait(ht.at[pl.ds(0, 11)], rsem.at[14])

    down = jnp.dot(wd_t[...], ht[...].reshape(NZ * HPAD, TOK), preferred_element_type=F32)
    rs2_send[...] = down.astype(BF).reshape(32, 16, TOK)

    def rs2_hop(i, carry):
        xp, yp, cp = plane_peer(i)
        send(rs2_send.at[yp * 8 + xp * 2 + cp], rs2_recv.at[me], 15, dev(xp, yp, z, cp))
        return carry

    lax.fori_loop(1, 32, rs2_hop, 0)
    rs2_recv[me] = rs2_send[y * 8 + x * 2 + c]

    @pl.when((x != y) | jnp.logical_not(owner))
    def _():
        wait(str_recv, rsem.at[12])

    wait(rs2_recv.at[pl.ds(0, 31)], rsem.at[15])
    result = str_recv[...].astype(F32) + jnp.sum(rs2_recv[...].astype(F32), axis=0)
    rounded = result.astype(BF)
    out_ref[0] = rounded[:, :REQ]
    out_ref[1] = rounded[:, REQ:]

    wait(ysend.at[pl.ds(0, 3)], ssem.at[0])
    wait(ystat.at[pl.ds(0, 3)], ssem.at[1])
    wait(zsend.at[pl.ds(0, 15)], ssem.at[2])
    wait(zrstat.at[pl.ds(0, 15)], ssem.at[3])
    wait(att.at[pl.ds(0, 15)], ssem.at[4])
    wait(rs1_send.at[pl.ds(0, 15)], ssem.at[5])
    wait(xt.at[:, pl.ds(0, 3)], ssem.at[7])
    wait(wg_recv.at[pl.ds(0, 7)], ssem.at[8])
    wait(wo_recv.at[pl.ds(0, 3)], ssem.at[10])
    wait(wd_recv.at[pl.ds(0, 3)], ssem.at[11])
    wait(gsend.at[pl.ds(0, 7)], ssem.at[13])
    wait(ht.at[pl.ds(0, 11)], ssem.at[14])
    wait(ht.at[0], ssem.at[16])
    wait(ht.at[0], ssem.at[17])
    wait(ht.at[0], ssem.at[18])
    wait(ht.at[0], ssem.at[19])
    wait(rs2_send.at[pl.ds(0, 31)], ssem.at[15])

    @pl.when(jnp.logical_not(owner))
    def _():
        wait(rs1_send.at[0], ssem.at[5])

    @pl.when(owner)
    def _():
        wait(xt.at[pl.ds(0, 5), pl.ds(0, 3)], ssem.at[6])

    @pl.when(owner & (x != y))
    def _():
        wait(res_recv, ssem.at[9])
        wait(res_recv, ssem.at[12])

    @pl.when(owner & (x == y))
    def _():
        wait(str_recv, ssem.at[12])


def body(
    resid,
    queries,
    new_kv,
    prefix_cache,
    suffix_cache,
    suffix_lengths,
    out_weight,
    norm_gain,
    gate_up,
    down_weight,
):
    hbm = pl.BlockSpec(memory_space=pl.ANY)
    vmem = pltpu.VMEM
    in_vmem = pl.BlockSpec(memory_space=vmem)
    result = pl.pallas_call(
        kernel,
        out_shape=jax.ShapeDtypeStruct((2, 16, REQ), BF),
        in_specs=[hbm] * 10,
        out_specs=in_vmem,
        scratch_shapes=[
            vmem((1, REQ), jnp.int32), vmem((2, 2, DH), BF), vmem((TOK, 128), BF),
            vmem((TOK, HEADS, DH), BF), vmem((TOK * HEADS, DH), F32), vmem((NY, DH, 2 * TOK), BF),
            vmem((KEYS, DH), BF), vmem((KEYS, DH), BF), vmem((DH, KEYS), BF), vmem((2, 8, DH), F32),
            vmem((128, TOK), BF),
            vmem((NY, 256, TOK), BF), vmem((NY, 8, TOK), F32), vmem((NY, 256, TOK), BF), vmem((NY, 8, TOK), F32),
            vmem((NZ, 16, TOK), BF), vmem((2, 2, TOK), F32), vmem((NZ, 16, TOK), BF), vmem((NZ, 2, TOK), F32),
            vmem((NZ, 16, TOK), BF),
            vmem((NY, 256, 128), BF), vmem((512, 256), BF), vmem((16, 32, TOK), BF), vmem((32, 32, TOK), BF),
            vmem((32, TOK), BF),
            vmem((8, NY, 32, TOK), BF), vmem((8, 112, ED), BF), vmem((8 * 112, ED), BF), vmem((1, ED), F32),
            vmem((8, 128, TOK), BF), vmem((8, 128, TOK), BF),
            vmem((NZ, HPAD, TOK), BF), vmem((NY, 896, 128), BF), vmem((512, NZ * HPAD), BF),
            vmem((32, 16, TOK), BF), vmem((32, 16, TOK), BF), vmem((16, TOK), BF),
            pltpu.SemaphoreType.DMA((12,)), pltpu.SemaphoreType.DMA((20,)), pltpu.SemaphoreType.DMA((20,)),
        ],
        compiler_params=pltpu.CompilerParams(
            collective_id=0, has_side_effects=True, vmem_limit_bytes=63 * 1024 * 1024
        ),
        name="layer",
    )(
        suffix_lengths.reshape(1, REQ), new_kv[:, 0, :, 0, :], resid.reshape(TOK, 128),
        queries.reshape(TOK, HEADS, DH), prefix_cache[:, :, 0, :], suffix_cache[:, 0, :, 0, :],
        out_weight, norm_gain.reshape(8, 1, ED), gate_up[:, :, 0, :].transpose(0, 2, 1).reshape(2 * HID, 8 * ED),
        down_weight,
    )
    return result.transpose(2, 0, 1)


def solution(mesh):
    placed = (
        P(None, None, "seq"),
        P(None, None, "kvh", None),
        P(None, "seq", None, "kvh", None),
        P(None, "seq", "kvh", None),
        P(None, "seq", None, "kvh", None),
        P(),
        P("kvh", "seq"),
        P(),
        P(None, None, "kvh", "seq"),
        P("kvh", "seq"),
    )
    return jax.shard_map(
        body, mesh=mesh, in_specs=placed, out_specs=P(None, None, ("seq", "kvh")), check_vma=False
    )
```

time: 96.7 us -> 80 us (0.83)
  Pallas kernels: 87.8 us -> 78.5 us
  local copies, waits for them, and re-layouts: 4.9 us -> 1.3 us
  other arithmetic: 3.47 us -> 0 us
    pallas_call x1, Pallas kernels: 87.8 us -> 78.5 us  [body(): pl.pallas_call(kernel, out_shape=jax.ShapeDtypeStruct((2, 16, REQ), BF),...]
    reshape x2 -> x0, local copies, waits for them, and re-layouts: 1.98 us -> none  [the longest x1 1.12 us: body(): q_t = rotated.transpose(2, 3, 1, 0).reshape(local_heads, head_dim, TOK)]
    convert_element_type x3 -> x0, other arithmetic: 1.03 us -> none  [the longest x2 1.02 us: rotate(): widened = values.astype(jnp.float32)]
    unnamed x22 -> x1, local copies, waits for them, and re-layouts: 2.22 us -> 1.3 us
where the time goes in v2:
time: 80 us; the launch traced here: 79.8 us
  Pallas kernels  78.5 us (98%)
  local copies, waits for them, and re-layouts  1.3 us (2%)
    pallas_call x1, Pallas kernels, body(): pl.pallas_call(kernel, out_shape=jax.ShapeDtypeStruct((2, 16, REQ), BF),...  78.5 us

profile of v2, /device:TPU:1, one launch (start us, length us, event | category | flops | bytes accessed | tf_op | source)
XLA Modules:
  0.0 79.8 jit_solution(1688397012648387629)
XLA Ops:
  0.0 78.5 %layer.1 = bf16[2,16,64]{2,1,0:T(8,128)(2,1)} custom-call(s32[1,64]{1,0:T(1,128)} %bitcast.21, bf16[2,2,128]{2,1,0:T(2,128)(2,1)} %bitcast.20, bf16[128,128]{1,0:T(8,128)(2,1)} %bitcast.17, bf16[128,8,128]{2,1,0:T(8,128)(2,1)} %bitcast.14, bf16[2,512,128]{2,1,0:T(8,128)(2,1)} %bitcast.15, bf16[2,256,128]{2,1,0:T(8,128)(2,1)} %bitcast.16, ...), custom_call_target="tpu_custom_call" | custom-call | tf_op jit(solution)/shard_map/layer/pallas_call | solution.py:473
  78.5 1.3 %copy.12 = bf16[64,2,16]{0,2,1:T(8,128)(2,1)} copy(bf16[64,2,16]{0,2,1:T(8,128)(2,1)} %bitcast.19) | data formatting | bytes 8192

commit v3 on v2

--- a/solution.py
+++ b/solution.py
@@ -24,6 +24,7 @@
 ED = 1024
 HID = 56
 HPAD = 64
+SX = 22
 BF, F32 = jnp.bfloat16, jnp.float32
 TN = (((0,), (0,)), ((), ()))
 
@@ -44,7 +45,7 @@
     out_ref,
     lens_ref, new_ref, res_ref, q_raw, q_wide, q_buf, k_buf, v_buf, vt_buf, new_buf, res_t,
     ysend, ystat, yrecv, yrstat,
-    zsend, zstat, zrecv, zrstat, att,
+    zsend, zstat, lrecv, lstat, hrecv, hstat, att,
     wo_recv, wo_t, rs1_send, rs1_recv, res_recv,
     xt, wg_recv, wg_buf, gain_buf, gsend, grecv,
     ht, wd_recv, wd_t, rs2_send, rs2_recv, str_recv,
@@ -54,12 +55,14 @@
     k = lax.axis_index("kvh")
     x, c = k // NC, k % NC
     y, z = s // NZ, s % NZ
+    zl, zh = z % 4, z // 4
     zc, zi = z // 8, z % 8
     owner = c == zc
 
-    def send(src, dst, stage, to):
+    def send(src, dst, stage, to, at=None):
+        at = stage if at is None else at
         copy = pltpu.make_async_remote_copy(
-            src_ref=src, dst_ref=dst, send_sem=ssem.at[stage], recv_sem=rsem.at[stage],
+            src_ref=src, dst_ref=dst, send_sem=ssem.at[stage], recv_sem=rsem.at[at],
             device_id=to, device_id_type=MESH,
         )
         copy.start()
@@ -67,11 +70,19 @@
     def wait(ref, sem):
         pltpu.make_async_copy(ref, ref, sem).wait()
 
-    def zpeer(i):
-        return (z + 8 + ((i + 1) // 2) * (1 - 2 * (i % 2))) % NZ
-
-    def plane_peer(i):
-        return (x + i // 8) % NX, (y + (i // 2) % NY) % NY, (c + i % 2) % NC
+    xs = [x] + [lax.rem(x + d, NX) for d in range(1, NX)]
+    ys = [y] + [lax.rem(y + d, NY) for d in range(1, NY)]
+    zs = [z] + [lax.rem(z + d, NZ) for d in range(1, NZ)]
+    cs = [c, 1 - c]
+    z_order = sorted(range(1, NZ), key=lambda d: -min(d, NZ - d))
+    zpeers = [(zs[d], dev(x, y, zs[d], c)) for d in z_order]
+    near = [(d, (zh * 4 + lax.rem(zl + d, 4))) for d in (2, 1, 3)]
+    near = [(zp % 4, dev(x, y, zp, c)) for _, zp in near]
+    far = [dev(x, y, lax.rem(zh + d, 4) * 4 + zl, c) for d in (2, 1, 3)]
+    plane = sorted(
+        [(i, j, l) for i in range(NX) for j in range(NY) for l in range(NC) if i + j + l],
+        key=lambda d: -(min(d[0], NX - d[0]) + min(d[1], NY - d[1])),
+    )
 
     load_q = pltpu.make_async_copy(q_hbm, q_raw, loc.at[0])
     load_q.start()
@@ -93,17 +104,13 @@
 
     barrier = pltpu.get_barrier_semaphore()
 
-    def greet_z(i, carry):
-        pl.semaphore_signal(barrier, inc=1, device_id=dev(x, y, zpeer(i), c), device_id_type=MESH)
-        return carry
-
-    def greet_plane(i, carry):
-        xp, yp, cp = plane_peer(i)
-        pl.semaphore_signal(barrier, inc=1, device_id=dev(xp, yp, z, cp), device_id_type=MESH)
-        return carry
-
-    lax.fori_loop(0, NZ - 1, greet_z, 0)
-    lax.fori_loop(1, 32, greet_plane, 0)
+    def greet(to):
+        pl.semaphore_signal(barrier, inc=1, device_id=to, device_id_type=MESH)
+
+    for _, to in zpeers:
+        greet(to)
+    for i, j, l in plane:
+        greet(dev(xs[i], ys[j], z, cs[l]))
     own_wg = pltpu.make_async_copy(wg_hbm.at[:, pl.ds(pl.multiple_of(k * ED, ED), ED)], wg_recv.at[k], loc.at[5])
     own_wo = pltpu.make_async_copy(wo_hbm.at[pl.ds(pl.multiple_of(y * 256, 256), 256)], wo_recv.at[y], loc.at[6])
     own_wd = pltpu.make_async_copy(wd_hbm.at[pl.ds(pl.multiple_of(y * 896, 896), 896)], wd_recv.at[y], loc.at[7])
@@ -172,25 +179,19 @@
         send(ysend.at[yp], yrecv.at[y], 0, dev(x, yp, z, c))
         send(ystat.at[yp], yrstat.at[y], 1, dev(x, yp, z, c))
 
-    first_y = (y + 2) % NY
-    attend(ysend.at[first_y], ystat.at[first_y], first_y)
+    for d in (2, 1, 3):
+        attend(ysend.at[ys[d]], ystat.at[ys[d]], ys[d])
     pl.semaphore_wait(barrier, 46)
-    y_send(first_y)
-
-    def wg_hop(d, carry):
-        kp = (k + d) % (NX * NC)
-        send(wg_hbm.at[:, pl.ds(pl.multiple_of(kp * ED, ED), ED)], wg_recv.at[k], 8, dev(kp // NC, y, z, kp % NC))
-        return carry
-
-    lax.fori_loop(1, NX * NC, wg_hop, 0)
-
-    def y_hop(d, carry):
-        yp = (y + 2 * d - 1) % NY
-        attend(ysend.at[yp], ystat.at[yp], yp)
-        y_send(yp)
-        return carry
-
-    lax.fori_loop(1, 3, y_hop, 0)
+    for d in (2, 1, 3):
+        y_send(ys[d])
+
+    for i in (2, 1, 3):
+        for l in range(NC):
+            kp = xs[i] * NC + cs[l]
+            send(wg_hbm.at[:, pl.ds(pl.multiple_of(kp * ED, ED), ED)], wg_recv.at[k], 8, dev(xs[i], y, z, cs[l]))
+    send(
+        wg_hbm.at[:, pl.ds(pl.multiple_of((x * NC + cs[1]) * ED, ED), ED)], wg_recv.at[k], 8, dev(x, y, z, cs[1])
+    )
 
     res_t[...] = lax.dot_general(res_ref[...], perm, TN, preferred_element_type=F32).astype(BF)
 
@@ -212,66 +213,61 @@
         facs = [jnp.exp(p - joint) for p in peaks]
         total = sum(yrstat[i, pl.ds(2 * h + 1, 1)] * facs[i] for i in range(NY))
         acc = sum(yrecv[i, pl.ds(h * DH, DH)].astype(F32) * facs[i] for i in range(NY))
-        zsend[pl.ds(h * 8, 8)] = acc.astype(BF).reshape(8, 16, TOK)
+        zsend[pl.ds(h * 2, 2)] = acc.astype(BF).reshape(2, 64, TOK)
         zstat[h, pl.ds(0, 1)] = joint
         zstat[h, pl.ds(1, 1)] = total
 
-    def z_hop(i, carry):
-        zp = zpeer(i)
-        send(zstat.at[zp // 8], zrstat.at[z], 3, dev(x, y, zp, c))
-        send(zsend.at[zp], zrecv.at[z], 2, dev(x, y, zp, c))
-        return carry
-
-    lax.fori_loop(0, NZ - 1, z_hop, 0)
-
-    def wo_hop(d, carry):
-        yp = (y + d) % NY
-        send(wo_hbm.at[pl.ds(pl.multiple_of(yp * 256, 256), 256)], wo_recv.at[y], 10, dev(x, yp, z, c))
-        return carry
-
-    def wd_hop(d, carry):
-        yp = (y + d) % NY
-        send(wd_hbm.at[pl.ds(pl.multiple_of(yp * 896, 896), 896)], wd_recv.at[y], 11, dev(x, yp, z, c))
-        return carry
-
-    lax.fori_loop(1, NY, wo_hop, 0)
-    lax.fori_loop(1, NY, wd_hop, 0)
-    zrecv[z] = zsend[z]
-    zrstat[z] = zstat[z // 8]
-    wait(zrstat.at[pl.ds(0, NZ - 1)], rsem.at[3])
-    wait(zrecv.at[pl.ds(0, NZ - 1)], rsem.at[2])
-
-    peaks = [zrstat[i, pl.ds(0, 1)] for i in range(NZ)]
-    joint = peaks[0]
-    for p in peaks[1:]:
-        joint = jnp.maximum(joint, p)
-    facs = [jnp.exp(p - joint) for p in peaks]
-    total = sum(zrstat[i, pl.ds(1, 1)] * facs[i] for i in range(NZ))
-    acc = sum(zrecv[i].astype(F32) * facs[i] for i in range(NZ))
-    att[z] = (acc / total).astype(BF)
-
-    def a_hop(i, carry):
-        send(att.at[z], att.at[z], 4, dev(x, y, zpeer(i), c))
-        return carry
-
-    lax.fori_loop(0, NZ - 1, a_hop, 0)
+    for zp, to in near:
+        send(zsend.at[zp], lrecv.at[zl], 2, to)
+        send(zstat.at[zp // 2], lstat.at[zl], 3, to)
+
+    for d in (2, 1, 3):
+        send(
+            wo_hbm.at[pl.ds(pl.multiple_of(ys[d] * 256, 256), 256)], wo_recv.at[y], 10, dev(x, ys[d], z, c)
+        )
+    for d in (2, 1, 3):
+        send(
+            wd_hbm.at[pl.ds(pl.multiple_of(ys[d] * 896, 896), 896)], wd_recv.at[y], 11, dev(x, ys[d], z, c)
+        )
+    lrecv[zl] = zsend[zl]
+    lstat[zl] = zstat[zl // 2]
+    wait(lstat.at[pl.ds(0, 3)], rsem.at[3])
+    wait(lrecv.at[pl.ds(0, 3)], rsem.at[2])
+
+    def joined(parts, stats):
+        peaks = [stats[i, pl.ds(0, 1)] for i in range(4)]
+        joint = jnp.maximum(jnp.maximum(peaks[0], peaks[1]), jnp.maximum(peaks[2], peaks[3]))
+        facs = [jnp.exp(p - joint) for p in peaks]
+        total = sum(stats[i, pl.ds(1, 1)] * facs[i] for i in range(4))
+        return joint, total, sum(parts[i].astype(F32) * facs[i] for i in range(4))
+
+    joint, total, acc = joined(lrecv, lstat)
+    hrecv[zh] = acc.astype(BF)
+    hstat[zh, pl.ds(0, 1)] = joint
+    hstat[zh, pl.ds(1, 1)] = total
+    for to in far:
+        send(hrecv.at[zh], hrecv.at[zh], 20, to)
+        send(hstat.at[zh], hstat.at[zh], 21, to)
+    wait(hstat.at[pl.ds(0, 3)], rsem.at[21])
+    wait(hrecv.at[pl.ds(0, 3)], rsem.at[20])
+    joint, total, acc = joined(hrecv, hstat)
+    att[zl] = (acc / total).astype(BF)
+    for _, to in near:
+        send(att.at[zl], att.at[zl], 4, to)
 
     own_wo.wait()
     wait(wo_recv.at[pl.ds(0, NY - 1)], rsem.at[10])
     for i in range(NY):
         wo_t[pl.ds(i * 128, 128)] = wo_recv[i].T
-    wait(att.at[pl.ds(0, NZ - 1)], rsem.at[4])
+    wait(att.at[pl.ds(0, 3)], rsem.at[4])
 
     proj = jnp.dot(wo_t[...], att[...].reshape(256, TOK), preferred_element_type=F32)
     rs1_send[...] = proj.astype(BF).reshape(16, 32, TOK)
     me = x * 8 + y * 2 + c
 
-    def rs1_hop(i, carry):
-        xp, yp = (x + i // 4) % NX, (y + i % 4) % NY
-        send(rs1_send.at[xp * 4 + yp], rs1_recv.at[me], 5, dev(xp, yp, z, zc))
-        return carry
-
-    lax.fori_loop(1, 16, rs1_hop, 0)
+    for i, j, l in plane:
+        if l == 0:
+            send(rs1_send.at[xs[i] * 4 + ys[j]], rs1_recv.at[me], 5, dev(xs[i], ys[j], z, zc))
 
     @pl.when(jnp.logical_not(owner))
     def _():
@@ -288,11 +284,10 @@
         summed = jnp.sum(rs1_recv[...].astype(F32), axis=0)
         xt[zi, y] = (res_recv[...].astype(F32) + summed).astype(BF)
 
-        def s_hop(i, carry):
-            send(xt.at[zi, y], xt.at[zi, y], 6, dev(x, y, zpeer(i), c))
-            return carry
-
-        lax.fori_loop(0, NZ - 1, s_hop, 0)
+        for _, to in zpeers:
+            send(xt.at[zi, y], xt.at[zi, y], 6, to, SX + zi)
+        for d in (2, 1, 3):
+            send(xt.at[zi, y], xt.at[zi, y], 7, dev(x, ys[d], z, c))
         for cp in range(NC):
             chunk = xt.at[zi, y, pl.ds(cp * 16, 16)]
 
@@ -304,6 +299,16 @@
             def _():
                 str_recv[...] = chunk[...]
 
+    up = (owner & (zi < 4)) | (jnp.logical_not(owner) & (zi >= 4))
+    for j in range(8):
+        i = jnp.where(up, j, 7 - j)
+
+        @pl.when(jnp.logical_not(owner) | (i != zi))
+        def _():
+            wait(xt.at[i, y], rsem.at[SX + i])
+            for d in (2, 1, 3):
+                send(xt.at[i, y], xt.at[i, y], 7, dev(x, ys[d], z, c))
+
     own_wg.wait()
     own_gain.wait()
     wait(wg_recv.at[pl.ds(0, 7)], rsem.at[8])
@@ -314,20 +319,6 @@
 
     lax.fori_loop(0, NX * NC, scale_gain, 0)
 
-    @pl.when(owner)
-    def _():
-        wait(xt.at[pl.ds(0, 7), 0], rsem.at[6])
-
-    @pl.when(jnp.logical_not(owner))
-    def _():
-        wait(xt.at[pl.ds(0, 8), 0], rsem.at[6])
-
-
-    def s2_hop(d, carry):
-        send(xt.at[:, y], xt.at[:, y], 7, dev(x, (y + d) % NY, z, c))
-        return carry
-
-    lax.fori_loop(1, NY, s2_hop, 0)
     wait(xt.at[:, pl.ds(0, 3)], rsem.at[7])
 
     stream = xt[...].reshape(ED, TOK)
@@ -341,12 +332,10 @@
     for i in range(8):
         gsend[i, pl.ds(112, 16)] = both
 
-    def g_hop(d, carry):
-        kp = (k + d) % (NX * NC)
-        send(gsend.at[kp], grecv.at[k], 13, dev(kp // NC, y, z, kp % NC))
-        return carry
-
-    lax.fori_loop(1, NX * NC, g_hop, 0)
+    for i in (2, 1, 3, 0):
+        for l in range(NC):
+            if i + l:
+                send(gsend.at[xs[i] * NC + cs[l]], grecv.at[k], 13, dev(xs[i], y, z, cs[l]))
     grecv[k] = gsend[k]
 
     own_wd.wait()
@@ -363,6 +352,7 @@
         return carry
 
     lax.fori_loop(0, NY, down_block, 0)
+
     wait(grecv.at[pl.ds(0, 7)], rsem.at[13])
     gu = jnp.sum(grecv[...].astype(F32), axis=0)
     inv_rms = lax.rsqrt((gu[112:113] + gu[113:114]) * (1.0 / (8 * ED)) + norm_eps)
@@ -372,14 +362,16 @@
     ht[z] = jnp.concatenate([hidden, jnp.zeros((HPAD - HID, TOK), F32)], axis=0).astype(BF)
 
     def zd(d):
-        return (z + d + NZ) % NZ
+        return zs[d % NZ]
 
     def h_send(block, d, stage):
         send(ht.at[block], ht.at[block], stage, dev(x, y, zd(d), c))
 
+    h_send(z, 8, 14)
     h_send(z, 5, 16)
     h_send(z, -5, 17)
-    h_send(z, 8, 14)
+    h_send(z, 7, 14)
+    h_send(z, -7, 14)
     h_send(z, 2, 18)
     h_send(z, -2, 19)
     h_send(z, 1, 14)
@@ -389,11 +381,9 @@
     wait(ht.at[0], rsem.at[19])
     h_send(zd(2), -1, 14)
     wait(ht.at[0], rsem.at[16])
-    h_send(zd(-5), 2, 14)
     h_send(zd(-5), 1, 14)
     h_send(zd(-5), -1, 14)
     wait(ht.at[0], rsem.at[17])
-    h_send(zd(5), -2, 14)
     h_send(zd(5), -1, 14)
     h_send(zd(5), 1, 14)
     wait(ht.at[pl.ds(0, 11)], rsem.at[14])
@@ -401,12 +391,8 @@
     down = jnp.dot(wd_t[...], ht[...].reshape(NZ * HPAD, TOK), preferred_element_type=F32)
     rs2_send[...] = down.astype(BF).reshape(32, 16, TOK)
 
-    def rs2_hop(i, carry):
-        xp, yp, cp = plane_peer(i)
-        send(rs2_send.at[yp * 8 + xp * 2 + cp], rs2_recv.at[me], 15, dev(xp, yp, z, cp))
-        return carry
-
-    lax.fori_loop(1, 32, rs2_hop, 0)
+    for i, j, l in plane:
+        send(rs2_send.at[ys[j] * 8 + xs[i] * 2 + cs[l]], rs2_recv.at[me], 15, dev(xs[i], ys[j], z, cs[l]))
     rs2_recv[me] = rs2_send[y * 8 + x * 2 + c]
 
     @pl.when((x != y) | jnp.logical_not(owner))
@@ -421,9 +407,11 @@
 
     wait(ysend.at[pl.ds(0, 3)], ssem.at[0])
     wait(ystat.at[pl.ds(0, 3)], ssem.at[1])
-    wait(zsend.at[pl.ds(0, 15)], ssem.at[2])
-    wait(zrstat.at[pl.ds(0, 15)], ssem.at[3])
-    wait(att.at[pl.ds(0, 15)], ssem.at[4])
+    wait(zsend.at[pl.ds(0, 3)], ssem.at[2])
+    wait(lstat.at[pl.ds(0, 3)], ssem.at[3])
+    wait(att.at[pl.ds(0, 3)], ssem.at[4])
+    wait(hrecv.at[pl.ds(0, 3)], ssem.at[20])
+    wait(hstat.at[pl.ds(0, 3)], ssem.at[21])
     wait(rs1_send.at[pl.ds(0, 15)], ssem.at[5])
     wait(xt.at[:, pl.ds(0, 3)], ssem.at[7])
     wait(wg_recv.at[pl.ds(0, 7)], ssem.at[8])
@@ -481,15 +469,15 @@
             vmem((KEYS, DH), BF), vmem((KEYS, DH), BF), vmem((DH, KEYS), BF), vmem((2, 8, DH), F32),
             vmem((128, TOK), BF),
             vmem((NY, 256, TOK), BF), vmem((NY, 8, TOK), F32), vmem((NY, 256, TOK), BF), vmem((NY, 8, TOK), F32),
-            vmem((NZ, 16, TOK), BF), vmem((2, 2, TOK), F32), vmem((NZ, 16, TOK), BF), vmem((NZ, 2, TOK), F32),
-            vmem((NZ, 16, TOK), BF),
+            vmem((4, 64, TOK), BF), vmem((2, 2, TOK), F32), vmem((4, 64, TOK), BF), vmem((4, 2, TOK), F32),
+            vmem((4, 64, TOK), BF), vmem((4, 2, TOK), F32), vmem((4, 64, TOK), BF),
             vmem((NY, 256, 128), BF), vmem((512, 256), BF), vmem((16, 32, TOK), BF), vmem((32, 32, TOK), BF),
             vmem((32, TOK), BF),
             vmem((8, NY, 32, TOK), BF), vmem((8, 112, ED), BF), vmem((8 * 112, ED), BF), vmem((1, ED), F32),
             vmem((8, 128, TOK), BF), vmem((8, 128, TOK), BF),
             vmem((NZ, HPAD, TOK), BF), vmem((NY, 896, 128), BF), vmem((512, NZ * HPAD), BF),
             vmem((32, 16, TOK), BF), vmem((32, 16, TOK), BF), vmem((16, TOK), BF),
-            pltpu.SemaphoreType.DMA((12,)), pltpu.SemaphoreType.DMA((20,)), pltpu.SemaphoreType.DMA((20,)),
+            pltpu.SemaphoreType.DMA((12,)), pltpu.SemaphoreType.DMA((22,)), pltpu.SemaphoreType.DMA((SX + 8,)),
         ],
         compiler_params=pltpu.CompilerParams(
             collective_id=0, has_side_effects=True, vmem_limit_bytes=63 * 1024 * 1024

time: 80 us -> 80.1 us (level)
  no operation moved by 1% of the time
where the time goes in v3:
time: 80.1 us; the launch traced here: 80 us
  Pallas kernels  78.7 us (98%)
  local copies, waits for them, and re-layouts  1.3 us (2%)
    pallas_call x1, Pallas kernels, body(): pl.pallas_call(kernel, out_shape=jax.ShapeDtypeStruct((2, 16, REQ), BF),...  78.7 us

profile of v3, /device:TPU:1, one launch (start us, length us, event | category | flops | bytes accessed | tf_op | source)
XLA Modules:
  0.0 80.0 jit_solution(4543785318183314808)
XLA Ops:
  0.0 78.7 %layer.1 = bf16[2,16,64]{2,1,0:T(8,128)(2,1)} custom-call(s32[1,64]{1,0:T(1,128)} %bitcast.21, bf16[2,2,128]{2,1,0:T(2,128)(2,1)} %bitcast.20, bf16[128,128]{1,0:T(8,128)(2,1)} %bitcast.17, bf16[128,8,128]{2,1,0:T(8,128)(2,1)} %bitcast.14, bf16[2,512,128]{2,1,0:T(8,128)(2,1)} %bitcast.15, bf16[2,256,128]{2,1,0:T(8,128)(2,1)} %bitcast.16, ...), custom_call_target="tpu_custom_call" | custom-call | tf_op jit(solution)/shard_map/layer/pallas_call | solution.py:461
  78.7 1.3 %copy.12 = bf16[64,2,16]{0,2,1:T(8,128)(2,1)} copy(bf16[64,2,16]{0,2,1:T(8,128)(2,1)} %bitcast.19) | data formatting | bytes 8192

commit v4 on v3

--- a/solution.py
+++ b/solution.py
@@ -45,7 +45,7 @@
     out_ref,
     lens_ref, new_ref, res_ref, q_raw, q_wide, q_buf, k_buf, v_buf, vt_buf, new_buf, res_t,
     ysend, ystat, yrecv, yrstat,
-    zsend, zstat, lrecv, lstat, hrecv, hstat, att,
+    zsend, zstat, zrecv, zrstat, att,
     wo_recv, wo_t, rs1_send, rs1_recv, res_recv,
     xt, wg_recv, wg_buf, gain_buf, gsend, grecv,
     ht, wd_recv, wd_t, rs2_send, rs2_recv, str_recv,
@@ -55,7 +55,6 @@
     k = lax.axis_index("kvh")
     x, c = k // NC, k % NC
     y, z = s // NZ, s % NZ
-    zl, zh = z % 4, z // 4
     zc, zi = z // 8, z % 8
     owner = c == zc
 
@@ -76,13 +75,20 @@
     cs = [c, 1 - c]
     z_order = sorted(range(1, NZ), key=lambda d: -min(d, NZ - d))
     zpeers = [(zs[d], dev(x, y, zs[d], c)) for d in z_order]
-    near = [(d, (zh * 4 + lax.rem(zl + d, 4))) for d in (2, 1, 3)]
-    near = [(zp % 4, dev(x, y, zp, c)) for _, zp in near]
-    far = [dev(x, y, lax.rem(zh + d, 4) * 4 + zl, c) for d in (2, 1, 3)]
     plane = sorted(
         [(i, j, l) for i in range(NX) for j in range(NY) for l in range(NC) if i + j + l],
         key=lambda d: -(min(d[0], NX - d[0]) + min(d[1], NY - d[1])),
     )
+
+    barrier = pltpu.get_barrier_semaphore()
+
+    def greet(to):
+        pl.semaphore_signal(barrier, inc=1, device_id=to, device_id_type=MESH)
+
+    for _, to in zpeers:
+        greet(to)
+    for i, j, l in plane:
+        greet(dev(xs[i], ys[j], z, cs[l]))
 
     load_q = pltpu.make_async_copy(q_hbm, q_raw, loc.at[0])
     load_q.start()
@@ -102,15 +108,6 @@
     for copy in loads:
         copy.start()
 
-    barrier = pltpu.get_barrier_semaphore()
-
-    def greet(to):
-        pl.semaphore_signal(barrier, inc=1, device_id=to, device_id_type=MESH)
-
-    for _, to in zpeers:
-        greet(to)
-    for i, j, l in plane:
-        greet(dev(xs[i], ys[j], z, cs[l]))
     own_wg = pltpu.make_async_copy(wg_hbm.at[:, pl.ds(pl.multiple_of(k * ED, ED), ED)], wg_recv.at[k], loc.at[5])
     own_wo = pltpu.make_async_copy(wo_hbm.at[pl.ds(pl.multiple_of(y * 256, 256), 256)], wo_recv.at[y], loc.at[6])
     own_wd = pltpu.make_async_copy(wd_hbm.at[pl.ds(pl.multiple_of(y * 896, 896), 896)], wd_recv.at[y], loc.at[7])
@@ -179,8 +176,12 @@
         send(ysend.at[yp], yrecv.at[y], 0, dev(x, yp, z, c))
         send(ystat.at[yp], yrstat.at[y], 1, dev(x, yp, z, c))
 
-    for d in (2, 1, 3):
-        attend(ysend.at[ys[d]], ystat.at[ys[d]], ys[d])
+    def attend_block(i, carry):
+        yq = lax.rem(y + 1 + i, NY)
+        attend(ysend.at[yq], ystat.at[yq], yq)
+        return carry
+
+    lax.fori_loop(0, NY - 1, attend_block, 0)
     pl.semaphore_wait(barrier, 46)
     for d in (2, 1, 3):
         y_send(ys[d])
@@ -213,13 +214,12 @@
         facs = [jnp.exp(p - joint) for p in peaks]
         total = sum(yrstat[i, pl.ds(2 * h + 1, 1)] * facs[i] for i in range(NY))
         acc = sum(yrecv[i, pl.ds(h * DH, DH)].astype(F32) * facs[i] for i in range(NY))
-        zsend[pl.ds(h * 2, 2)] = acc.astype(BF).reshape(2, 64, TOK)
-        zstat[h, pl.ds(0, 1)] = joint
-        zstat[h, pl.ds(1, 1)] = total
-
-    for zp, to in near:
-        send(zsend.at[zp], lrecv.at[zl], 2, to)
-        send(zstat.at[zp // 2], lstat.at[zl], 3, to)
+        zsend[pl.ds(h * 8, 8)] = (acc / total).astype(BF).reshape(8, 16, TOK)
+        zstat[h] = joint + jnp.log(total)
+
+    for zp, to in zpeers:
+        send(zstat.at[zp // 8], zrstat.at[z], 3, to)
+        send(zsend.at[zp], zrecv.at[z], 2, to)
 
     for d in (2, 1, 3):
         send(
@@ -229,49 +229,46 @@
         send(
             wd_hbm.at[pl.ds(pl.multiple_of(ys[d] * 896, 896), 896)], wd_recv.at[y], 11, dev(x, ys[d], z, c)
         )
-    lrecv[zl] = zsend[zl]
-    lstat[zl] = zstat[zl // 2]
-    wait(lstat.at[pl.ds(0, 3)], rsem.at[3])
-    wait(lrecv.at[pl.ds(0, 3)], rsem.at[2])
-
-    def joined(parts, stats):
-        peaks = [stats[i, pl.ds(0, 1)] for i in range(4)]
-        joint = jnp.maximum(jnp.maximum(peaks[0], peaks[1]), jnp.maximum(peaks[2], peaks[3]))
-        facs = [jnp.exp(p - joint) for p in peaks]
-        total = sum(stats[i, pl.ds(1, 1)] * facs[i] for i in range(4))
-        return joint, total, sum(parts[i].astype(F32) * facs[i] for i in range(4))
-
-    joint, total, acc = joined(lrecv, lstat)
-    hrecv[zh] = acc.astype(BF)
-    hstat[zh, pl.ds(0, 1)] = joint
-    hstat[zh, pl.ds(1, 1)] = total
-    for to in far:
-        send(hrecv.at[zh], hrecv.at[zh], 20, to)
-        send(hstat.at[zh], hstat.at[zh], 21, to)
-    wait(hstat.at[pl.ds(0, 3)], rsem.at[21])
-    wait(hrecv.at[pl.ds(0, 3)], rsem.at[20])
-    joint, total, acc = joined(hrecv, hstat)
-    att[zl] = (acc / total).astype(BF)
-    for _, to in near:
-        send(att.at[zl], att.at[zl], 4, to)
+    zrecv[z] = zsend[z]
+    zrstat[z] = zstat[z // 8]
+    wait(zrstat.at[pl.ds(0, NZ - 1)], rsem.at[3])
+    wait(zrecv.at[pl.ds(0, NZ - 1)], rsem.at[2])
+
+    logs = [zrstat[i] for i in range(NZ)]
+    joint = logs[0]
+    for p in logs[1:]:
+        joint = jnp.maximum(joint, p)
+    facs = [jnp.exp(p - joint) for p in logs]
+    acc = sum(zrecv[i].astype(F32) * facs[i] for i in range(NZ))
+    att[z] = (acc / sum(facs)).astype(BF)
+
+    for _, to in zpeers:
+        send(att.at[z], att.at[z], 4, to)
 
     own_wo.wait()
     wait(wo_recv.at[pl.ds(0, NY - 1)], rsem.at[10])
     for i in range(NY):
         wo_t[pl.ds(i * 128, 128)] = wo_recv[i].T
-    wait(att.at[pl.ds(0, 3)], rsem.at[4])
-
-    proj = jnp.dot(wo_t[...], att[...].reshape(256, TOK), preferred_element_type=F32)
-    rs1_send[...] = proj.astype(BF).reshape(16, 32, TOK)
+    wait(att.at[pl.ds(0, NZ - 1)], rsem.at[4])
+
     me = x * 8 + y * 2 + c
-
-    for i, j, l in plane:
-        if l == 0:
-            send(rs1_send.at[xs[i] * 4 + ys[j]], rs1_recv.at[me], 5, dev(xs[i], ys[j], z, zc))
-
-    @pl.when(jnp.logical_not(owner))
-    def _():
-        send(rs1_send.at[x * 4 + y], rs1_recv.at[me], 5, dev(x, y, z, zc))
+    spread = att[...].reshape(256, TOK)
+
+    def project(i, carry):
+        xp = lax.rem(x + 2 + i, NX)
+        rows = pl.ds(pl.multiple_of(xp * 128, 128), 128)
+        proj = jnp.dot(wo_t[rows], spread, preferred_element_type=F32)
+        rs1_send[pl.ds(xp * 4, 4)] = proj.astype(BF).reshape(4, 32, TOK)
+        for j in (2, 1, 3):
+            send(rs1_send.at[xp * 4 + ys[j]], rs1_recv.at[me], 5, dev(xp, ys[j], z, zc))
+
+        @pl.when((xp != x) | jnp.logical_not(owner))
+        def _():
+            send(rs1_send.at[xp * 4 + y], rs1_recv.at[me], 5, dev(xp, y, z, zc))
+
+        return carry
+
+    lax.fori_loop(0, NX, project, 0)
 
     @pl.when(owner & (x != y))
     def _():
@@ -322,20 +319,26 @@
     wait(xt.at[:, pl.ds(0, 3)], rsem.at[7])
 
     stream = xt[...].reshape(ED, TOK)
-    part = jnp.dot(wg_buf[...], stream, preferred_element_type=F32)
-    gsend[:, pl.ds(0, 112)] = part.astype(BF).reshape(8, 112, TOK)
     wide = stream.astype(F32)
     squares = jnp.sum(wide * wide, axis=0, keepdims=True)
     high = squares.astype(BF).astype(F32)
     row16 = lax.broadcasted_iota(jnp.int32, (16, TOK), 0)
     both = jnp.where(row16 == 0, high, jnp.where(row16 == 1, squares - high, 0.0)).astype(BF)
-    for i in range(8):
-        gsend[i, pl.ds(112, 16)] = both
-
-    for i in (2, 1, 3, 0):
-        for l in range(NC):
-            if i + l:
-                send(gsend.at[xs[i] * NC + cs[l]], grecv.at[k], 13, dev(xs[i], y, z, cs[l]))
+    def gate_up_block(i, carry):
+        kp = lax.rem(k + 4 + i, NX * NC)
+        part = jnp.dot(
+            wg_buf[pl.ds(pl.multiple_of(kp * 112, 112), 112)], stream, preferred_element_type=F32
+        )
+        gsend[kp, pl.ds(0, 112)] = part.astype(BF)
+        gsend[kp, pl.ds(112, 16)] = both
+
+        @pl.when(kp != k)
+        def _():
+            send(gsend.at[kp], grecv.at[k], 13, dev(kp // NC, y, z, kp % NC))
+
+        return carry
+
+    lax.fori_loop(0, NX * NC, gate_up_block, 0)
     grecv[k] = gsend[k]
 
     own_wd.wait()
@@ -367,11 +370,9 @@
     def h_send(block, d, stage):
         send(ht.at[block], ht.at[block], stage, dev(x, y, zd(d), c))
 
-    h_send(z, 8, 14)
     h_send(z, 5, 16)
     h_send(z, -5, 17)
-    h_send(z, 7, 14)
-    h_send(z, -7, 14)
+    h_send(z, 8, 14)
     h_send(z, 2, 18)
     h_send(z, -2, 19)
     h_send(z, 1, 14)
@@ -381,18 +382,35 @@
     wait(ht.at[0], rsem.at[19])
     h_send(zd(2), -1, 14)
     wait(ht.at[0], rsem.at[16])
+    h_send(zd(-5), 2, 14)
     h_send(zd(-5), 1, 14)
     h_send(zd(-5), -1, 14)
     wait(ht.at[0], rsem.at[17])
+    h_send(zd(5), -2, 14)
     h_send(zd(5), -1, 14)
     h_send(zd(5), 1, 14)
     wait(ht.at[pl.ds(0, 11)], rsem.at[14])
 
-    down = jnp.dot(wd_t[...], ht[...].reshape(NZ * HPAD, TOK), preferred_element_type=F32)
-    rs2_send[...] = down.astype(BF).reshape(32, 16, TOK)
-
-    for i, j, l in plane:
-        send(rs2_send.at[ys[j] * 8 + xs[i] * 2 + cs[l]], rs2_recv.at[me], 15, dev(xs[i], ys[j], z, cs[l]))
+    gathered = ht[...].reshape(NZ * HPAD, TOK)
+
+    def down_project(i, carry):
+        yp = lax.rem(y + 2 + i, NY)
+        down = jnp.dot(
+            wd_t[pl.ds(pl.multiple_of(yp * 128, 128), 128)], gathered, preferred_element_type=F32
+        )
+        rs2_send[pl.ds(yp * 8, 8)] = down.astype(BF).reshape(8, 16, TOK)
+        for i in (2, 1, 3):
+            for l in range(NC):
+                send(rs2_send.at[yp * 8 + xs[i] * 2 + cs[l]], rs2_recv.at[me], 15, dev(xs[i], yp, z, cs[l]))
+        send(rs2_send.at[yp * 8 + x * 2 + cs[1]], rs2_recv.at[me], 15, dev(x, yp, z, cs[1]))
+
+        @pl.when(yp != y)
+        def _():
+            send(rs2_send.at[yp * 8 + k], rs2_recv.at[me], 15, dev(x, yp, z, c))
+
+        return carry
+
+    lax.fori_loop(0, NY, down_project, 0)
     rs2_recv[me] = rs2_send[y * 8 + x * 2 + c]
 
     @pl.when((x != y) | jnp.logical_not(owner))
@@ -407,11 +425,9 @@
 
     wait(ysend.at[pl.ds(0, 3)], ssem.at[0])
     wait(ystat.at[pl.ds(0, 3)], ssem.at[1])
-    wait(zsend.at[pl.ds(0, 3)], ssem.at[2])
-    wait(lstat.at[pl.ds(0, 3)], ssem.at[3])
-    wait(att.at[pl.ds(0, 3)], ssem.at[4])
-    wait(hrecv.at[pl.ds(0, 3)], ssem.at[20])
-    wait(hstat.at[pl.ds(0, 3)], ssem.at[21])
+    wait(zsend.at[pl.ds(0, 15)], ssem.at[2])
+    wait(zrstat.at[pl.ds(0, 15)], ssem.at[3])
+    wait(att.at[pl.ds(0, 15)], ssem.at[4])
     wait(rs1_send.at[pl.ds(0, 15)], ssem.at[5])
     wait(xt.at[:, pl.ds(0, 3)], ssem.at[7])
     wait(wg_recv.at[pl.ds(0, 7)], ssem.at[8])
@@ -469,8 +485,8 @@
             vmem((KEYS, DH), BF), vmem((KEYS, DH), BF), vmem((DH, KEYS), BF), vmem((2, 8, DH), F32),
             vmem((128, TOK), BF),
             vmem((NY, 256, TOK), BF), vmem((NY, 8, TOK), F32), vmem((NY, 256, TOK), BF), vmem((NY, 8, TOK), F32),
-            vmem((4, 64, TOK), BF), vmem((2, 2, TOK), F32), vmem((4, 64, TOK), BF), vmem((4, 2, TOK), F32),
-            vmem((4, 64, TOK), BF), vmem((4, 2, TOK), F32), vmem((4, 64, TOK), BF),
+            vmem((NZ, 16, TOK), BF), vmem((2, 1, TOK), F32), vmem((NZ, 16, TOK), BF), vmem((NZ, 1, TOK), F32),
+            vmem((NZ, 16, TOK), BF),
             vmem((NY, 256, 128), BF), vmem((512, 256), BF), vmem((16, 32, TOK), BF), vmem((32, 32, TOK), BF),
             vmem((32, TOK), BF),
             vmem((8, NY, 32, TOK), BF), vmem((8, 112, ED), BF), vmem((8 * 112, ED), BF), vmem((1, ED), F32),

time: 80.1 us -> 76.9 us (0.960)
  Pallas kernels: 78.7 us -> 75.5 us
    pallas_call x1, Pallas kernels: 78.7 us -> 75.5 us  [body(): pl.pallas_call(kernel, out_shape=jax.ShapeDtypeStruct((2, 16, REQ), BF),...]
where the time goes in v4:
time: 76.9 us; the launch traced here: 76.8 us
  Pallas kernels  75.5 us (98%)
  local copies, waits for them, and re-layouts  1.3 us (2%)
    pallas_call x1, Pallas kernels, body(): pl.pallas_call(kernel, out_shape=jax.ShapeDtypeStruct((2, 16, REQ), BF),...  75.5 us

profile of v4, /device:TPU:1, one launch (start us, length us, event | category | flops | bytes accessed | tf_op | source)
XLA Modules:
  0.0 76.8 jit_solution(2071276178613408332)
XLA Ops:
  0.0 75.5 %layer.1 = bf16[2,16,64]{2,1,0:T(8,128)(2,1)} custom-call(s32[1,64]{1,0:T(1,128)} %bitcast.21, bf16[2,2,128]{2,1,0:T(2,128)(2,1)} %bitcast.20, bf16[128,128]{1,0:T(8,128)(2,1)} %bitcast.17, bf16[128,8,128]{2,1,0:T(8,128)(2,1)} %bitcast.14, bf16[2,512,128]{2,1,0:T(8,128)(2,1)} %bitcast.15, bf16[2,256,128]{2,1,0:T(8,128)(2,1)} %bitcast.16, ...), custom_call_target="tpu_custom_call" | custom-call | tf_op jit(solution)/shard_map/layer/pallas_call | solution.py:477
  75.5 1.3 %copy.12 = bf16[64,2,16]{0,2,1:T(8,128)(2,1)} copy(bf16[64,2,16]{0,2,1:T(8,128)(2,1)} %bitcast.19) | data formatting | bytes 8192

commit v5 on v4

--- a/solution.py
+++ b/solution.py
@@ -234,13 +234,10 @@
     wait(zrstat.at[pl.ds(0, NZ - 1)], rsem.at[3])
     wait(zrecv.at[pl.ds(0, NZ - 1)], rsem.at[2])
 
-    logs = [zrstat[i] for i in range(NZ)]
-    joint = logs[0]
-    for p in logs[1:]:
-        joint = jnp.maximum(joint, p)
-    facs = [jnp.exp(p - joint) for p in logs]
-    acc = sum(zrecv[i].astype(F32) * facs[i] for i in range(NZ))
-    att[z] = (acc / sum(facs)).astype(BF)
+    logs = zrstat[...].reshape(NZ, TOK)
+    facs = jnp.exp(logs - jnp.max(logs, axis=0, keepdims=True))
+    acc = jnp.sum(zrecv[...].astype(F32) * facs[:, None, :], axis=0)
+    att[z] = (acc / jnp.sum(facs, axis=0, keepdims=True)).astype(BF)
 
     for _, to in zpeers:
         send(att.at[z], att.at[z], 4, to)
@@ -255,7 +252,7 @@
     spread = att[...].reshape(256, TOK)
 
     def project(i, carry):
-        xp = lax.rem(x + 2 + i, NX)
+        xp = xs[(2, 3, 1, 0)[i]]
         rows = pl.ds(pl.multiple_of(xp * 128, 128), 128)
         proj = jnp.dot(wo_t[rows], spread, preferred_element_type=F32)
         rs1_send[pl.ds(xp * 4, 4)] = proj.astype(BF).reshape(4, 32, TOK)
@@ -268,7 +265,8 @@
 
         return carry
 
-    lax.fori_loop(0, NX, project, 0)
+    for block in range(4):
+        project(block, 0)
 
     @pl.when(owner & (x != y))
     def _():
@@ -338,7 +336,8 @@
 
         return carry
 
-    lax.fori_loop(0, NX * NC, gate_up_block, 0)
+    for block in range(8):
+        gate_up_block(block, 0)
     grecv[k] = gsend[k]
 
     own_wd.wait()
@@ -372,16 +371,14 @@
 
     h_send(z, 5, 16)
     h_send(z, -5, 17)
-    h_send(z, 8, 14)
-    h_send(z, 2, 18)
-    h_send(z, -2, 19)
-    h_send(z, 1, 14)
-    h_send(z, -1, 14)
+    h_send(z, 1, 18)
+    h_send(z, -1, 19)
     wait(ht.at[0], rsem.at[18])
-    h_send(zd(-2), 1, 14)
+    h_send(zd(-1), 1, 20)
     wait(ht.at[0], rsem.at[19])
-    h_send(zd(2), -1, 14)
+    h_send(zd(1), -1, 21)
     wait(ht.at[0], rsem.at[16])
+    h_send(zd(-5), 3, 14)
     h_send(zd(-5), 2, 14)
     h_send(zd(-5), 1, 14)
     h_send(zd(-5), -1, 14)
@@ -389,12 +386,16 @@
     h_send(zd(5), -2, 14)
     h_send(zd(5), -1, 14)
     h_send(zd(5), 1, 14)
-    wait(ht.at[pl.ds(0, 11)], rsem.at[14])
+    wait(ht.at[0], rsem.at[20])
+    h_send(zd(-2), 1, 14)
+    wait(ht.at[0], rsem.at[21])
+    h_send(zd(2), -1, 14)
+    wait(ht.at[pl.ds(0, 9)], rsem.at[14])
 
     gathered = ht[...].reshape(NZ * HPAD, TOK)
 
     def down_project(i, carry):
-        yp = lax.rem(y + 2 + i, NY)
+        yp = ys[(2, 3, 1, 0)[i]]
         down = jnp.dot(
             wd_t[pl.ds(pl.multiple_of(yp * 128, 128), 128)], gathered, preferred_element_type=F32
         )
@@ -410,18 +411,13 @@
 
         return carry
 
-    lax.fori_loop(0, NY, down_project, 0)
+    for block in range(4):
+        down_project(block, 0)
     rs2_recv[me] = rs2_send[y * 8 + x * 2 + c]
 
     @pl.when((x != y) | jnp.logical_not(owner))
     def _():
         wait(str_recv, rsem.at[12])
-
-    wait(rs2_recv.at[pl.ds(0, 31)], rsem.at[15])
-    result = str_recv[...].astype(F32) + jnp.sum(rs2_recv[...].astype(F32), axis=0)
-    rounded = result.astype(BF)
-    out_ref[0] = rounded[:, :REQ]
-    out_ref[1] = rounded[:, REQ:]
 
     wait(ysend.at[pl.ds(0, 3)], ssem.at[0])
     wait(ystat.at[pl.ds(0, 3)], ssem.at[1])
@@ -434,11 +430,13 @@
     wait(wo_recv.at[pl.ds(0, 3)], ssem.at[10])
     wait(wd_recv.at[pl.ds(0, 3)], ssem.at[11])
     wait(gsend.at[pl.ds(0, 7)], ssem.at[13])
-    wait(ht.at[pl.ds(0, 11)], ssem.at[14])
+    wait(ht.at[pl.ds(0, 9)], ssem.at[14])
     wait(ht.at[0], ssem.at[16])
     wait(ht.at[0], ssem.at[17])
     wait(ht.at[0], ssem.at[18])
     wait(ht.at[0], ssem.at[19])
+    wait(ht.at[0], ssem.at[20])
+    wait(ht.at[0], ssem.at[21])
     wait(rs2_send.at[pl.ds(0, 31)], ssem.at[15])
 
     @pl.when(jnp.logical_not(owner))
@@ -457,6 +455,12 @@
     @pl.when(owner & (x == y))
     def _():
         wait(str_recv, ssem.at[12])
+
+    wait(rs2_recv.at[pl.ds(0, 31)], rsem.at[15])
+    result = str_recv[...].astype(F32) + jnp.sum(rs2_recv[...].astype(F32), axis=0)
+    rounded = result.astype(BF)
+    out_ref[0] = rounded[:, :REQ]
+    out_ref[1] = rounded[:, REQ:]
 
 
 def body(
@@ -484,7 +488,7 @@
             vmem((TOK, HEADS, DH), BF), vmem((TOK * HEADS, DH), F32), vmem((NY, DH, 2 * TOK), BF),
             vmem((KEYS, DH), BF), vmem((KEYS, DH), BF), vmem((DH, KEYS), BF), vmem((2, 8, DH), F32),
             vmem((128, TOK), BF),
-            vmem((NY, 256, TOK), BF), vmem((NY, 8, TOK), F32), vmem((NY, 256, TOK), BF), vmem((NY, 8, TOK), F32),
+            vmem((NY, 256, TOK), BF), vmem((NY, 4, TOK), F32), vmem((NY, 256, TOK), BF), vmem((NY, 4, TOK), F32),
             vmem((NZ, 16, TOK), BF), vmem((2, 1, TOK), F32), vmem((NZ, 16, TOK), BF), vmem((NZ, 1, TOK), F32),
             vmem((NZ, 16, TOK), BF),
             vmem((NY, 256, 128), BF), vmem((512, 256), BF), vmem((16, 32, TOK), BF), vmem((32, 32, TOK), BF),

time: 76.9 us -> 76.7 us (level)
  no operation moved by 1% of the time
where the time goes in v5:
time: 76.7 us; the launch traced here: 76.6 us
  Pallas kernels  75.3 us (98%)
  local copies, waits for them, and re-layouts  1.3 us (2%)
    pallas_call x1, Pallas kernels, body(): pl.pallas_call(kernel, out_shape=jax.ShapeDtypeStruct((2, 16, REQ), BF),...  75.3 us

profile of v5, /device:TPU:1, one launch (start us, length us, event | category | flops | bytes accessed | tf_op | source)
XLA Modules:
  0.0 76.6 jit_solution(13055107545929891399)
XLA Ops:
  0.0 75.3 %layer.1 = bf16[2,16,64]{2,1,0:T(8,128)(2,1)} custom-call(s32[1,64]{1,0:T(1,128)} %bitcast.21, bf16[2,2,128]{2,1,0:T(2,128)(2,1)} %bitcast.20, bf16[128,128]{1,0:T(8,128)(2,1)} %bitcast.17, bf16[128,8,128]{2,1,0:T(8,128)(2,1)} %bitcast.14, bf16[2,512,128]{2,1,0:T(8,128)(2,1)} %bitcast.15, bf16[2,256,128]{2,1,0:T(8,128)(2,1)} %bitcast.16, ...), custom_call_target="tpu_custom_call" | custom-call | tf_op jit(solution)/shard_map/layer/pallas_call | solution.py:481
  75.3 1.3 %copy.12 = bf16[64,2,16]{0,2,1:T(8,128)(2,1)} copy(bf16[64,2,16]{0,2,1:T(8,128)(2,1)} %bitcast.19) | data formatting | bytes 8192

commit v6 on v5

--- a/solution.py
+++ b/solution.py
@@ -186,14 +186,16 @@
     for d in (2, 1, 3):
         y_send(ys[d])
 
-    for i in (2, 1, 3):
-        for l in range(NC):
-            kp = xs[i] * NC + cs[l]
-            send(wg_hbm.at[:, pl.ds(pl.multiple_of(kp * ED, ED), ED)], wg_recv.at[k], 8, dev(xs[i], y, z, cs[l]))
-    send(
-        wg_hbm.at[:, pl.ds(pl.multiple_of((x * NC + cs[1]) * ED, ED), ED)], wg_recv.at[k], 8, dev(x, y, z, cs[1])
-    )
-
+    def wg_rows(n, carry):
+        rows = pl.ds(pl.multiple_of(n * 16, 16), 16)
+        for i in (2, 1, 3, 0):
+            for l in range(NC):
+                if i + l:
+                    lanes = pl.ds(pl.multiple_of((xs[i] * NC + cs[l]) * ED, ED), ED)
+                    send(wg_hbm.at[rows, lanes], wg_recv.at[k, rows], 8, dev(xs[i], y, z, cs[l]))
+        return carry
+
+    lax.fori_loop(0, 7, wg_rows, 0)
     res_t[...] = lax.dot_general(res_ref[...], perm, TN, preferred_element_type=F32).astype(BF)
 
     @pl.when(owner & (x != y))
@@ -323,16 +325,16 @@
     row16 = lax.broadcasted_iota(jnp.int32, (16, TOK), 0)
     both = jnp.where(row16 == 0, high, jnp.where(row16 == 1, squares - high, 0.0)).astype(BF)
     def gate_up_block(i, carry):
-        kp = lax.rem(k + 4 + i, NX * NC)
+        kp = xs[(2, 2, 1, 1, 3, 3, 0, 0)[i]] * NC + cs[(0, 1, 0, 1, 0, 1, 1, 0)[i]]
         part = jnp.dot(
             wg_buf[pl.ds(pl.multiple_of(kp * 112, 112), 112)], stream, preferred_element_type=F32
         )
         gsend[kp, pl.ds(0, 112)] = part.astype(BF)
         gsend[kp, pl.ds(112, 16)] = both
 
-        @pl.when(kp != k)
-        def _():
-            send(gsend.at[kp], grecv.at[k], 13, dev(kp // NC, y, z, kp % NC))
+        if i < 7:
+            to = dev(xs[(2, 2, 1, 1, 3, 3, 0)[i]], y, z, cs[(0, 1, 0, 1, 0, 1, 1)[i]])
+            send(gsend.at[kp], grecv.at[k], 13, to)
 
         return carry
 

time: 76.7 us -> 75.9 us (0.990)
  Pallas kernels: 75.3 us -> 74.4 us
    pallas_call x1, Pallas kernels: 75.3 us -> 74.4 us  [body(): pl.pallas_call(kernel, out_shape=jax.ShapeDtypeStruct((2, 16, REQ), BF),...]
where the time goes in v6:
time: 75.9 us; the launch traced here: 75.7 us
  Pallas kernels  74.4 us (98%)
  local copies, waits for them, and re-layouts  1.3 us (2%)
    pallas_call x1, Pallas kernels, body(): pl.pallas_call(kernel, out_shape=jax.ShapeDtypeStruct((2, 16, REQ), BF),...  74.4 us

profile of v6, /device:TPU:1, one launch (start us, length us, event | category | flops | bytes accessed | tf_op | source)
XLA Modules:
  0.0 75.7 jit_solution(13839799081807041439)
XLA Ops:
  0.0 74.4 %layer.1 = bf16[2,16,64]{2,1,0:T(8,128)(2,1)} custom-call(s32[1,64]{1,0:T(1,128)} %bitcast.21, bf16[2,2,128]{2,1,0:T(2,128)(2,1)} %bitcast.20, bf16[128,128]{1,0:T(8,128)(2,1)} %bitcast.17, bf16[128,8,128]{2,1,0:T(8,128)(2,1)} %bitcast.14, bf16[2,512,128]{2,1,0:T(8,128)(2,1)} %bitcast.15, bf16[2,256,128]{2,1,0:T(8,128)(2,1)} %bitcast.16, ...), custom_call_target="tpu_custom_call" | custom-call | tf_op jit(solution)/shard_map/layer/pallas_call | solution.py:483
  74.4 1.3 %copy.12 = bf16[64,2,16]{0,2,1:T(8,128)(2,1)} copy(bf16[64,2,16]{0,2,1:T(8,128)(2,1)} %bitcast.19) | data formatting | bytes 8192

commit v7 on v6

--- a/solution.py
+++ b/solution.py
@@ -172,9 +172,6 @@
             stat[pl.ds(2 * h, 1)] = peak[:, h * TOK : (h + 1) * TOK]
             stat[pl.ds(2 * h + 1, 1)] = total[:, h * TOK : (h + 1) * TOK]
 
-    def y_send(yp):
-        send(ysend.at[yp], yrecv.at[y], 0, dev(x, yp, z, c))
-        send(ystat.at[yp], yrstat.at[y], 1, dev(x, yp, z, c))
 
     def attend_block(i, carry):
         yq = lax.rem(y + 1 + i, NY)
@@ -184,7 +181,9 @@
     lax.fori_loop(0, NY - 1, attend_block, 0)
     pl.semaphore_wait(barrier, 46)
     for d in (2, 1, 3):
-        y_send(ys[d])
+        send(ysend.at[ys[d]], yrecv.at[y], 0, dev(x, ys[d], z, c))
+    for d in (2, 1, 3):
+        send(ystat.at[ys[d]], yrstat.at[y], 1, dev(x, ys[d], z, c))
 
     def wg_rows(n, carry):
         rows = pl.ds(pl.multiple_of(n * 16, 16), 16)
@@ -220,8 +219,8 @@
         zstat[h] = joint + jnp.log(total)
 
     for zp, to in zpeers:
+        send(zsend.at[zp], zrecv.at[z], 2, to)
         send(zstat.at[zp // 8], zrstat.at[z], 3, to)
-        send(zsend.at[zp], zrecv.at[z], 2, to)
 
     for d in (2, 1, 3):
         send(

time: 75.9 us -> 77 us (1.014)
  Pallas kernels: 74.4 us -> 75.5 us
    pallas_call x1, Pallas kernels: 74.4 us -> 75.5 us  [body(): pl.pallas_call(kernel, out_shape=jax.ShapeDtypeStruct((2, 16, REQ), BF),...]
where the time goes in v7:
time: 77 us; the launch traced here: 76.8 us
  Pallas kernels  75.5 us (98%)
  local copies, waits for them, and re-layouts  1.3 us (2%)
    pallas_call x1, Pallas kernels, body(): pl.pallas_call(kernel, out_shape=jax.ShapeDtypeStruct((2, 16, REQ), BF),...  75.5 us

profile of v7, /device:TPU:1, one launch (start us, length us, event | category | flops | bytes accessed | tf_op | source)
XLA Modules:
  0.0 76.8 jit_solution(1825957728631516278)
XLA Ops:
  0.0 75.5 %layer.1 = bf16[2,16,64]{2,1,0:T(8,128)(2,1)} custom-call(s32[1,64]{1,0:T(1,128)} %bitcast.21, bf16[2,2,128]{2,1,0:T(2,128)(2,1)} %bitcast.20, bf16[128,128]{1,0:T(8,128)(2,1)} %bitcast.17, bf16[128,8,128]{2,1,0:T(8,128)(2,1)} %bitcast.14, bf16[2,512,128]{2,1,0:T(8,128)(2,1)} %bitcast.15, bf16[2,256,128]{2,1,0:T(8,128)(2,1)} %bitcast.16, ...), custom_call_target="tpu_custom_call" | custom-call | tf_op jit(solution)/shard_map/layer/pallas_call | solution.py:482
  75.5 1.3 %copy.12 = bf16[64,2,16]{0,2,1:T(8,128)(2,1)} copy(bf16[64,2,16]{0,2,1:T(8,128)(2,1)} %bitcast.19) | data formatting | bytes 8192
